TPU v7x, 256 devices: a whole 4x4x8 slice. The times are simulated.
256 devices in a mesh: island: 16 (over x, z_lo, core), fsdp: 16 (over z_hi, y).
Axes of the slice: x: 4, y: 4, z: 8 (z_hi: 4, z_lo: 2; z = z_hi * 2 + z_lo), core: 2. Of those that a mesh axis runs over, the one named last changes fastest.
Arguments:
- pseudo_grads: float32 [16, 256, 28672], P('island', 'fsdp'), may hold values from -6 to 6
- master_slab: float32 [256, 28672], P('fsdp', 'island'), may hold values from -6 to 6
- momentum: float32 [256, 28672], P('fsdp', 'island'), may hold values from -3 to 3
- inner_inputs: bfloat16 [65536, 8192], P(('island', 'fsdp')), may hold values from -6 to 6
- token_ids: int32 [65536], P(('island', 'fsdp')), may hold values from 0 to 31999, as said below
- inner_weight: bfloat16 [16, 512, 8192], P('island', 'fsdp'), may hold values from -0.0625 to 0.0625
- readout: float32 [512], replicated, may hold values from -5 to 5
Outputs:
- new_slab: bfloat16 [256, 28672], P('fsdp')
- master_new: float32 [256, 28672], P('fsdp', 'island')
- momentum_new: float32 [256, 28672], P('fsdp', 'island')
- weight_grad: float32 [16, 512, 8192], P('island', 'fsdp')
- input_grad: bfloat16 [65536, 8192], P(('island', 'fsdp'))
Inputs may be any that keep to these rules, and one draw needn't show every extreme that they name: `token_ids`: 0 marks a padding token; other values are token ids.
All inputs are finite; a program needn't handle non-finite values.
Results may differ from a plain program's by a relative error of at most 0.0049.
Values may be sent and summed in bfloat16 or wider, within the bound.
A program may use at most 128 MiB of HBM per device.

v0:
```python
import math

import jax
import jax.numpy as jnp
from jax import lax
from jax.sharding import PartitionSpec as P


def silu_slope(pre):
    sig = jax.nn.sigmoid(pre)
    return sig * (1.0 + pre * (1.0 - sig))


def outer_update(pseudo_grads, master_slab, momentum):
    replicas = lax.axis_size("island")
    summed = lax.psum_scatter(pseudo_grads, "island", scatter_dimension=2, tiled=True)
    mean_delta = summed[0] / replicas
    momentum_new = 0.9 * momentum + mean_delta
    master_new = master_slab - 0.7 * (mean_delta + 0.9 * momentum_new)
    owned = master_new.astype(jnp.bfloat16)
    new_slab = lax.all_gather(owned, "island", axis=1, tiled=True)
    return (new_slab, master_new, momentum_new)


def inner_pass(inner_inputs, token_ids, inner_weight, readout):
    weight = inner_weight[0]
    shard_tokens = inner_inputs.shape[0]
    groups = lax.axis_size("fsdp")
    scale = 1.0 / math.sqrt(shard_tokens * groups)
    keep = (token_ids != 0).astype(jnp.float32)
    rows = lax.all_gather(weight, "fsdp", axis=0, tiled=True)
    pre = jnp.einsum("tk,fk->tf", inner_inputs, rows, preferred_element_type=jnp.float32)
    slope = (scale * keep[:, None] * readout[None, :] * silu_slope(pre)).astype(jnp.bfloat16)
    back = jnp.dot(slope, rows, preferred_element_type=jnp.float32)
    slopes, back = (slope, back)
    grad_rows = lax.psum_scatter(
        jnp.einsum("tf,tk->fk", slopes, inner_inputs, preferred_element_type=jnp.float32),
        "fsdp",
        scatter_dimension=0,
        tiled=True,
    )
    return (grad_rows[None], back.astype(jnp.bfloat16))


def on_device(pseudo_grads, master_slab, momentum, inner_inputs, token_ids, inner_weight, readout):
    weight_grad, input_grad = inner_pass(inner_inputs, token_ids, inner_weight, readout)
    new_slab, master_new, momentum_new = outer_update(pseudo_grads, master_slab, momentum)
    return (new_slab, master_new, momentum_new, weight_grad, input_grad)


def solution(mesh):
    in_specs = (
        P("island", "fsdp", None),
        P("fsdp", "island"),
        P("fsdp", "island"),
        P(("island", "fsdp"), None),
        P(("island", "fsdp")),
        P("island", "fsdp", None),
        P(),
    )
    out_specs = (
        P("fsdp", None),
        P("fsdp", "island"),
        P("fsdp", "island"),
        P("island", "fsdp", None),
        P(("island", "fsdp"), None),
    )
    return jax.shard_map(
        on_device, mesh=mesh, in_specs=in_specs, out_specs=out_specs, check_vma=False
    )
```

profile of v0, /device:TPU:22, one launch (start us, length us, event | category | flops | bytes accessed | tf_op | source)
XLA Modules:
  0.0 373.8 jit_solution(12277451617310919139)
XLA Ops:
  8.0 0.0 all-gather.3.cloned.1.call-start
  8.0 0.7 all-gather.3.cloned.1.call-update
  8.7 0.0 copy-start.3
  8.7 0.0 reduce-scatter.3.cloned.1.call-start
  8.8 0.5 reduce-scatter.3.cloned.1.call-update
  9.3 0.0 reduce-scatter.5.cloned.1.call-start
  9.4 0.7 compare_select_fusion
  10.1 127.2 %all-gather.3.cloned.1.call-done = bf16[1,512,8192]{2,1,0:T(8,128)(2,1)} async-done(((bf16[1,32,8192]{2,1,0:T(8,128)(2,1)}), bf16[1,512,8192]{2,1,0:T(8,128)(2,1)}) %all-gather.3.cloned.1.call-update) | async-done | bytes 8388624 | tf_op jit(solution)/shard_map/all_gather | solution.py:31
  137.2 0.0 copy-start
  137.2 7.2 %fusion.1 = f32[256,512]{1,0:T(8,128)S(1)} fusion(bf16[256,8192]{1,0:T(8,128)(2,1)} %param.10, bf16[1,512,8192]{2,1,0:T(8,128)(2,1)} %all-gather.3.cloned.1.call-done), kind=kOutput, calls=%fused_computation.2 | convolution fusion | flops 2147483648 | bytes 13107200 | tf_op jit(solution)/shard_map/tk,fk->tf/dot_general | solution.py:32
  144.4 0.0 copy-done.3
  144.4 0.0 copy-done
  144.4 8.3 %fusion.3 = f32[512,8192]{1,0:T(8,128)} fusion(bf16[256,8192]{1,0:T(8,128)(2,1)S(1)} %copy-done, f32[256,512]{1,0:T(8,128)S(1)} %fusion.1, f32[512]{0:T(512)S(1)} %copy-done.3, f32[256]{0:T(256)S(1)} %compare_select_fusion), kind=kOutput, calls=%fused_computation.5 | convolution fusion | flops 2148794368 | bytes 21498880 | tf_op jit(solution)/shard_map/tf,tk->fk/dot_general | solution.py:37
  152.7 0.0 copy-start.1
  152.7 0.0 copy-start.2
  152.7 0.0 reduce-scatter.5.cloned.1.call-update
  152.8 0.0 reduce-scatter.3.cloned.1.call-done
  152.8 0.8 copy-done.1
  153.6 0.1 copy-done.2
  153.7 1.6 fusion.16
  155.3 25.9 %all_gather.6 = bf16[16,28672]{1,0:T(8,128)(2,1)S(1)} all-gather(bf16[16,1792]{1,0:T(8,128)(2,1)S(1)} %get-tuple-element.5), channel_id=1, replica_groups=mesh['island'=16,'fsdp'=16] {'island'}, dimensions={1}, use_global_device_ids=true | all-gather | bytes 974848 | tf_op jit(solution)/shard_map/all_gather | solution.py:21
  181.2 8.0 %convolution_convert_fusion = bf16[256,8192]{1,0:T(8,128)(2,1)} fusion(bf16[1,512,8192]{2,1,0:T(8,128)(2,1)} %all-gather.3.cloned.1.call-done, f32[256,512]{1,0:T(8,128)S(1)} %fusion.1, f32[512]{0:T(512)S(1)} %copy-done.3, f32[256]{0:T(256)S(1)} %compare_select_fusion), kind=kOutput, calls=%fused_computation | convolution fusion | flops 2150891520 | bytes 13110272 | tf_op jit(solution)/shard_map/dot_general | solution.py:34
  189.2 176.3 %reduce-scatter.5.cloned.1.call-done = f32[32,8192]{1,0:T(8,128)} async-done(((f32[512,8192]{1,0:T(8,128)}), f32[32,8192]{1,0:T(8,128)}) %reduce-scatter.5.cloned.1.call-update) | async-done | bytes 1048592 | tf_op jit(solution)/shard_map/reduce_scatter | solution.py:36
  365.4 0.9 copy.13
Async XLA Ops:
  8.0 129.2 %all-gather.3.cloned.1.call-start = ((), (), s32[]{:S(2)}) async-start(), calls=%async_computation.4 | async-start | bytes 8912896 | tf_op jit(solution)/shard_map/all_gather | solution.py:31
  8.7 135.7 %copy-start.3 = (f32[512]{0:T(512)S(1)}, f32[512]{0:T(512)}, u32[]{:S(2)}) copy-start(f32[512]{0:T(512)} %param.13) | copy-start | bytes 6148
  8.7 144.0 %reduce-scatter.3.cloned.1.call-start = ((), (), s32[]{:S(2)}) async-start(), calls=%async_computation.2 | async-start | bytes 1949696 | tf_op jit(solution)/shard_map/reduce_scatter | solution.py:16
  9.3 356.1 %reduce-scatter.5.cloned.1.call-start = ((), (), s32[]{:S(2)}) async-start(), calls=%async_computation.3 | async-start | bytes 17825792 | tf_op jit(solution)/shard_map/reduce_scatter | solution.py:36
  137.2 7.2 %copy-start = (bf16[256,8192]{1,0:T(8,128)(2,1)S(1)}, bf16[256,8192]{1,0:T(8,128)(2,1)}, u32[]{:S(2)}) copy-start(bf16[256,8192]{1,0:T(8,128)(2,1)} %param.10) | copy-start | bytes 12582916
  152.7 0.9 copy-start.1
  152.7 1.0 copy-start.2
Sparse Core Ops, SparseCore 0:
  11.6 125.5 all-gather.2
Sparse Core Ops, SparseCore 1:
  11.8 132.0 reduce-scatter.2
  152.8 212.5 reduce-scatter.4
where the time goes:
time: 375 us; the launch traced here: 374 us
  waiting for transfers between devices  305 us (81%)
  blocking collectives  25.9 us (7%)
  matrix products  23.5 us (6%)
  between operations  15.5 us (4%)
    reduce_scatter x1, waiting for transfers between devices, inner_pass(): lax.psum_scatter(jnp.einsum('tf,tk->fk', slopes, inner_inputs, preferred_...  176 us
    all_gather x1, waiting for transfers between devices, inner_pass(): rows = lax.all_gather(weight, 'fsdp', axis=0, tiled=True)  127 us
    all_gather x1, blocking collectives, outer_update(): new_slab = lax.all_gather(owned, 'island', axis=1, tiled=True)  25.9 us
    dot_general x1, matrix products, inner_pass(): jnp.einsum('tf,tk->fk', slopes, inner_inputs, preferred_element_type=jnp....  8.3 us
    dot_general x1, matrix products, inner_pass(): back = jnp.dot(slope, rows, preferred_element_type=jnp.float32)  7.99 us
  transfers between devices with their start and end apart: 3, of which 2 were waited for; matrix products, arithmetic and copies ran while one was open for 7% of the time, Pallas kernels for 0%

commit v1 on v0

v1 whole, which is shorter than its diff:
```python
import math

import jax
import jax.numpy as jnp
from jax import lax
from jax.experimental import pallas as pl
from jax.experimental.pallas import tpu as pltpu
from jax.sharding import PartitionSpec as P

MESH = pl.DeviceIdType.MESH
F32, BF16 = jnp.float32, jnp.bfloat16
N_SEMS = 96


def kernel(
    groups, share, scale,
    pg, master, momentum, xin, tok, w, readout,
    slab_out, master_out, momentum_out, wg_out, dx_out,
    xb, wv, dwp, snd, slt, sl, dxb, tokb, rob, pre,
    ra1, ra0, rt1, rt0, ru1, ru0, rv1, rv0,
    acc, rc, rx, rz, msb, mob, slab,
    ssem, rsem, lsem, gsem,
):
    f, i = lax.axis_index("fsdp"), lax.axis_index("island")
    h, y = f // 4, lax.rem(f, 4)
    x, z, c = i // 4, lax.rem(i // 2, 2), lax.rem(i, 2)

    def at_y(d):
        return {"fsdp": h * 4 + lax.rem(y + d, 4)}

    def at_h(d):
        return {"fsdp": lax.rem(h + d, 4) * 4 + y}

    def at_x(d):
        return {"island": lax.rem(x + d, 4) * 4 + z * 2 + c}

    at_z = {"island": x * 4 + (1 - z) * 2 + c}
    at_c = {"island": x * 4 + z * 2 + 1 - c}

    k = xb.shape[1]
    r = w.shape[1]
    g = r * 4
    ka = share
    kb = k - ka
    ha, hb = ka // 2, kb // 2
    A, A1, A2 = pl.ds(0, ka), pl.ds(0, ha), pl.ds(ha, ha)
    B, B1, B2 = pl.ds(ka, kb), pl.ds(ka, hb), pl.ds(ka + hb, hb)

    def rows(dh, dy):
        return pl.ds(pl.multiple_of(dh * g + lax.rem(y + dy, 4) * r, r), r)

    def group(dh):
        return pl.ds(dh * g, g)

    copies = {}

    def send(name, src, dst, device):
        n = len(copies)
        copies[name] = pltpu.make_async_remote_copy(
            src_ref=src, dst_ref=dst, send_sem=ssem.at[n], recv_sem=rsem.at[n],
            device_id=device, device_id_type=MESH,
        )
        copies[name].start()

    def got(*names):
        for name in names:
            copies[name].wait_recv()

    loads = []

    def load(src, dst, n):
        cp = pltpu.make_async_copy(src, dst, lsem.at[n])
        cp.start()
        loads.append(cp)
        return cp

    cols = slab.shape[1] // groups

    def block(n):
        return pl.ds(pl.multiple_of(n * cols, 128), cols)

    lx = load(xin, xb, 0)
    lw = load(w.at[0], wv.at[rows(0, 0)], 1)
    lt = load(tok, tokb, 2)
    lr = load(readout, rob, 3)
    lms = load(master, msb, 4)
    lmo = load(momentum, mob, 5)
    for j in range(8):
        pltpu.make_async_copy(pg.at[0, :, block(2 * j + c)], acc.at[j], lsem.at[6]).start()

    barrier = pltpu.get_barrier_semaphore()
    partners = [at_y(1), at_y(3), at_h(1), at_h(3), at_x(1), at_x(2), at_x(3), at_z, at_c]
    for device in partners:
        pl.semaphore_signal(barrier, inc=1, device_id=device, device_id_type=MESH)
    pl.semaphore_wait(barrier, len(partners))

    own = rows(0, 0)
    send("Ah+", w.at[0, :, A], wv.at[rows(3, 0), A], at_h(1))
    send("Ah-", w.at[0, :, A], wv.at[rows(1, 0), A], at_h(3))
    send("By+", w.at[0, :, B], wv.at[own, B], at_y(1))
    send("By-", w.at[0, :, B], wv.at[own, B], at_y(3))
    send("Ay+0", w.at[0, :, A], wv.at[own, A], at_y(1))
    send("Ay-0", w.at[0, :, A], wv.at[own, A], at_y(3))
    for j in range(8):
        pltpu.make_async_remote_copy(
            src_ref=pg.at[0, :, block(2 * j + 1 - c)], dst_ref=rc.at[j], send_sem=gsem.at[0], recv_sem=gsem.at[1],
            device_id=at_c, device_id_type=MESH,
        ).start()

    def all_blocks(n, ref):
        return pltpu.make_async_remote_copy(
            src_ref=ref, dst_ref=ref, send_sem=gsem.at[n], recv_sem=gsem.at[n + 1], device_id=at_c, device_id_type=MESH
        )

    def pre_part(dh, lo, n, step, start):
        def body(j, total):
            at = pl.ds(pl.multiple_of(lo + j * step, 128), step)
            return total + lax.dot_general(
                wv[group(dh), at], xb[:, at], (((1,), (1,)), ((), ())), preferred_element_type=F32
            )

        return lax.fori_loop(0, n // step, body, start)

    def pre_a(dh):
        pre[group(dh)] = pre_part(dh, 0, ka, ka // 5, jnp.zeros((g, xb.shape[0]), F32))

    def slope(dh):
        p = pre_part(dh, ka, kb, kb, pre[group(dh)])
        sig = jax.nn.sigmoid(p)
        keep = (tokb[...] != 0).astype(F32)
        row = rob[pl.ds(lax.rem(h + dh, 4), 1), :]
        column = jnp.transpose(jnp.broadcast_to(row, (g, g)))
        weight = jnp.concatenate([column] * (xb.shape[0] // g), axis=1)
        s = scale * keep * weight * (sig * (1.0 + p * (1.0 - sig)))
        slt[group(dh)] = s.astype(BF16)
        sl[:, group(dh)] = jnp.transpose(s).astype(BF16)

    def dw(dh, lo, n, step):
        s = slt[group(dh)]

        def body(j, carry):
            at = pl.ds(pl.multiple_of(lo + j * step, 128), step)
            part = jnp.dot(s, xb[:, at], preferred_element_type=F32)
            dwp[group(dh), at] = part
            snd[group(dh), at] = part.astype(BF16)
            return carry

        lax.fori_loop(0, n // step, body, 0)

    def dw_all(dh):
        dw(dh, 0, ka, ka // 5)
        dw(dh, ka, kb, kb)

    def add(at_rows, lo, n, terms, step, keep=False, out=True):
        def body(j, carry):
            at = pl.ds(pl.multiple_of(lo + j * step, 128), step)
            total = dwp[at_rows, at]
            for ref, off in terms:
                total = total + ref[:, pl.ds(pl.multiple_of(lo - off + j * step, 128), step)].astype(F32)
            if keep:
                dwp[at_rows, at] = total
            if out:
                snd[at_rows, at] = total.astype(BF16)
            return carry

        lax.fori_loop(0, n // step, body, 0)

    sa, sb = ka // 10, kb // 2

    got("By+", "By-")
    send("Byf+", wv.at[rows(0, 3), B1], wv.at[rows(0, 3), B1], at_y(1))
    send("Byf-", wv.at[rows(0, 1), B2], wv.at[rows(0, 1), B2], at_y(3))

    pltpu.make_async_copy(acc, acc, lsem.at[6]).wait()
    all_blocks(0, rc).wait_recv()
    for j in range(8):
        acc[j] = acc[j] + rc[j]
    for d in (1, 3, 2):
        send(f"X{d}", acc.at[pl.ds(lax.rem(x + d, 4) * 2, 2)], rx.at[d - 1], at_x(d))

    got("Ay+0", "Ay-0")
    send("Ayf+0", wv.at[rows(0, 3), A1], wv.at[rows(0, 3), A1], at_y(1))
    send("Ayf-0", wv.at[rows(0, 1), A2], wv.at[rows(0, 1), A2], at_y(3))
    got("Byf+", "Byf-")
    lw.wait()

    got("Ah+", "Ah-")
    send("Ay+3", wv.at[rows(3, 0), A], wv.at[rows(3, 0), A], at_y(1))
    send("Ay-3", wv.at[rows(3, 0), A], wv.at[rows(3, 0), A], at_y(3))
    send("Ay+1", wv.at[rows(1, 0), A], wv.at[rows(1, 0), A], at_y(1))
    send("Ay-1", wv.at[rows(1, 0), A], wv.at[rows(1, 0), A], at_y(3))
    send("Ahf+", wv.at[rows(3, 0), A1], wv.at[rows(2, 0), A1], at_h(1))
    send("Ahf-", wv.at[rows(1, 0), A2], wv.at[rows(2, 0), A2], at_h(3))
    send("Bh+", wv.at[group(0), B], wv.at[group(3), B], at_h(1))
    send("Bh-", wv.at[group(0), B], wv.at[group(1), B], at_h(3))

    got("X1", "X3", "X2")
    two = acc.at[pl.ds(x * 2, 2)]
    two[...] = two[...] + rx[0] + rx[1] + rx[2]
    send("Z", acc.at[x * 2 + 1 - z], rz, at_z)

    got("Ayf+0", "Ayf-0")
    lx.wait()
    lt.wait()
    lr.wait()
    pre_a(0)
    slope(0)
    got("Ay+3", "Ay-3")
    send("Ayf+3", wv.at[rows(3, 3), A1], wv.at[rows(3, 3), A1], at_y(1))
    send("Ayf-3", wv.at[rows(3, 1), A2], wv.at[rows(3, 1), A2], at_y(3))
    got("Ahf+", "Ahf-")
    send("Ay+2", wv.at[rows(2, 0), A], wv.at[rows(2, 0), A], at_y(1))
    send("Ay-2", wv.at[rows(2, 0), A], wv.at[rows(2, 0), A], at_y(3))
    dw_all(0)

    got("Z")
    lms.wait()
    lmo.wait()
    mean = (acc[x * 2 + z] + rz[...]) / groups
    mob[...] = 0.9 * mob[...] + mean
    msb[...] = msb[...] - 0.7 * (mean + 0.9 * mob[...])
    mine = block(i)
    slab[:, mine] = msb[...].astype(BF16)
    send("SZ", slab.at[:, mine], slab.at[:, mine], at_z)
    load(msb, master_out, 7)
    load(mob, momentum_out, 8)

    got("Ay+1", "Ay-1")
    send("Ayf+1", wv.at[rows(1, 3), A1], wv.at[rows(1, 3), A1], at_y(1))
    send("Ayf-1", wv.at[rows(1, 1), A2], wv.at[rows(1, 1), A2], at_y(3))
    got("SZ")
    other = block(x * 4 + (1 - z) * 2 + c)
    for d in (1, 3, 2):
        send(f"SX{d}", slab.at[:, mine], slab.at[:, mine], at_x(d))
        send(f"SY{d}", slab.at[:, other], slab.at[:, other], at_x(d))
    got("Ayf+3", "Ayf-3")
    pre_a(3)
    got("Bh+", "Bh-")
    send("Bhf+", wv.at[group(3), B1], wv.at[group(2), B1], at_h(1))
    send("Bhf-", wv.at[group(1), B2], wv.at[group(2), B2], at_h(3))
    slope(3)
    got("Ayf+1", "Ayf-1")
    pre_a(1)
    got("Ay+2", "Ay-2")
    send("Ayf+2", wv.at[rows(2, 3), A1], wv.at[rows(2, 3), A1], at_y(1))
    send("Ayf-2", wv.at[rows(2, 1), A2], wv.at[rows(2, 1), A2], at_y(3))
    slope(1)
    dw_all(3)
    dw_all(1)
    got("SX1", "SX3", "SX2", "SY1", "SY3", "SY2")
    for j in range(8):
        at = block(2 * j + c)
        pltpu.make_async_remote_copy(
            src_ref=slab.at[:, at], dst_ref=slab.at[:, at], send_sem=gsem.at[2], recv_sem=gsem.at[3],
            device_id=at_c, device_id_type=MESH,
        ).start()

    def s1(d):
        send(f"S1+{d}", snd.at[rows(d, 2), A1], ra1.at[0, d], at_y(1))
        send(f"S1-{d}", snd.at[rows(d, 2), A2], ra1.at[1, d], at_y(3))

    def s2(d):
        send(f"S2+{d}", snd.at[rows(d, 1), A2], ra0.at[0, d, :, A2], at_y(1))
        send(f"S2-{d}", snd.at[rows(d, 3), A1], ra0.at[1, d, :, A1], at_y(3))

    def s3(d):
        got(f"S1+{d}", f"S1-{d}")
        add(rows(d, 1), 0, ha, [(ra1.at[0, d], 0)], sa)
        add(rows(d, 3), ha, ha, [(ra1.at[1, d], ha)], sa)
        send(f"S3+{d}", snd.at[rows(d, 1), A1], ra0.at[0, d, :, A1], at_y(1))
        send(f"S3-{d}", snd.at[rows(d, 3), A2], ra0.at[1, d, :, A2], at_y(3))

    def sum_a(d):
        got(f"S2+{d}", f"S2-{d}", f"S3+{d}", f"S3-{d}")
        add(rows(d, 0), 0, ka, [(ra0.at[0, d], 0), (ra0.at[1, d], 0)], sa, keep=True, out=d != 0)

    send("U2+", snd.at[group(1), B2], ru0.at[0, :, pl.ds(hb, hb)], at_h(1))
    send("U2-", snd.at[group(3), B1], ru0.at[1, :, pl.ds(0, hb)], at_h(3))
    s1(1)
    s1(3)
    got("Bhf+", "Bhf-")
    got("Ayf+2", "Ayf-2")
    pre_a(2)
    slope(2)
    dw_all(2)
    s1(2)
    s2(2)
    send("U1+", snd.at[group(2), B1], ru1.at[0], at_h(1))
    send("U1-", snd.at[group(2), B2], ru1.at[1], at_h(3))
    s2(1)
    s2(3)

    def dx(j, carry):
        at = pl.ds(pl.multiple_of(j * 512, 128), 512)
        dxb[:, at] = jnp.dot(sl[...], wv[:, at], preferred_element_type=F32).astype(BF16)
        return carry

    lax.fori_loop(0, k // 512, dx, 0)
    load(dxb, dx_out, 9)
    s3(2)
    s3(1)
    s3(3)
    s1(0)
    s2(0)
    got("U1+", "U1-")
    add(group(1), ka, hb, [(ru1.at[0], ka)], sb)
    add(group(3), ka + hb, hb, [(ru1.at[1], ka + hb)], sb)
    send("U3+", snd.at[group(1), B1], ru0.at[0, :, pl.ds(0, hb)], at_h(1))
    send("U3-", snd.at[group(3), B2], ru0.at[1, :, pl.ds(hb, hb)], at_h(3))
    all_blocks(2, slab.at[:, pl.ds(0, slab.shape[1] // 2)]).wait_recv()
    load(slab, slab_out, 10)
    sum_a(2)
    send("T1+", snd.at[rows(2, 0), A1], rt1.at[0], at_h(1))
    send("T1-", snd.at[rows(2, 0), A2], rt1.at[1], at_h(3))
    sum_a(1)
    send("T2+", snd.at[rows(1, 0), A2], rt0.at[0, :, A2], at_h(1))
    sum_a(3)
    send("T2-", snd.at[rows(3, 0), A1], rt0.at[1, :, A1], at_h(3))
    s3(0)
    got("U2+", "U2-", "U3+", "U3-")
    add(group(0), ka, kb, [(ru0.at[0], ka), (ru0.at[1], ka)], sb, keep=True)
    send("V1+", snd.at[rows(0, 2), B1], rv1.at[0], at_y(1))
    send("V1-", snd.at[rows(0, 2), B2], rv1.at[1], at_y(3))
    send("V2+", snd.at[rows(0, 1), B2], rv0.at[0, :, pl.ds(hb, hb)], at_y(1))
    send("V2-", snd.at[rows(0, 3), B1], rv0.at[1, :, pl.ds(0, hb)], at_y(3))
    got("T1+", "T1-")
    add(rows(1, 0), 0, ha, [(rt1.at[0], 0)], sa)
    add(rows(3, 0), ha, ha, [(rt1.at[1], ha)], sa)
    send("T3+", snd.at[rows(1, 0), A1], rt0.at[0, :, A1], at_h(1))
    send("T3-", snd.at[rows(3, 0), A2], rt0.at[1, :, A2], at_h(3))
    got("V1+", "V1-")
    add(rows(0, 1), ka, hb, [(rv1.at[0], ka)], sb)
    add(rows(0, 3), ka + hb, hb, [(rv1.at[1], ka + hb)], sb)
    send("V3+", snd.at[rows(0, 1), B1], rv0.at[0, :, pl.ds(0, hb)], at_y(1))
    send("V3-", snd.at[rows(0, 3), B2], rv0.at[1, :, pl.ds(hb, hb)], at_y(3))
    sum_a(0)
    got("V2+", "V2-", "V3+", "V3-")
    add(own, ka, kb, [(rv0.at[0], ka), (rv0.at[1], ka)], sb, keep=True, out=False)
    got("T2+", "T2-", "T3+", "T3-")
    add(own, 0, ka, [(rt0.at[0], 0), (rt0.at[1], 0)], sa, keep=True, out=False)
    load(dwp.at[own], wg_out.at[0], 11)

    for copy in copies.values():
        copy.wait_send()
    all_blocks(0, rc).wait_send()
    all_blocks(2, slab.at[:, pl.ds(0, slab.shape[1] // 2)]).wait_send()
    for cp in loads[6:]:
        cp.wait()


def on_device(pseudo_grads, master_slab, momentum, inner_inputs, token_ids, inner_weight, readout):
    groups = lax.axis_size("island")
    tokens, k = inner_inputs.shape
    r = inner_weight.shape[1]
    features = readout.shape[0]
    g = 4 * r
    width, cols = pseudo_grads.shape[2], master_slab.shape[1]
    out_rows = pseudo_grads.shape[1]
    share = (k // 256) * 25 // 32 * 256
    ka, kb = share, k - share
    ha, hb = ka // 2, kb // 2
    scale = 1.0 / math.sqrt(tokens * lax.axis_size("fsdp"))
    V, sem = pltpu.VMEM, pltpu.SemaphoreType.DMA
    anywhere = pl.BlockSpec(memory_space=pl.ANY)

    def body(*refs):
        kernel(groups, share, scale, *refs)

    return pl.pallas_call(
        body,
        out_shape=(
            jax.ShapeDtypeStruct((out_rows, width), BF16),
            jax.ShapeDtypeStruct(master_slab.shape, F32),
            jax.ShapeDtypeStruct(momentum.shape, F32),
            jax.ShapeDtypeStruct((1, r, k), F32),
            jax.ShapeDtypeStruct((tokens, k), BF16),
        ),
        in_specs=[anywhere] * 7,
        out_specs=[anywhere] * 5,
        scratch_shapes=[
            V((tokens, k), BF16),
            V((features, k), BF16),
            V((features, k), F32),
            V((features, k), BF16),
            V((features, tokens), BF16),
            V((tokens, features), BF16),
            V((tokens, k), BF16),
            V((1, tokens), jnp.int32),
            V((4, g), F32),
            V((features, tokens), F32),
            V((2, 4, r, ha), BF16),
            V((2, 4, r, ka), BF16),
            V((2, r, ha), BF16),
            V((2, r, ka), BF16),
            V((2, g, hb), BF16),
            V((2, g, kb), BF16),
            V((2, r, hb), BF16),
            V((2, r, kb), BF16),
            V((8, out_rows, cols), F32),
            V((8, out_rows, cols), F32),
            V((3, 2, out_rows, cols), F32),
            V((out_rows, cols), F32),
            V((out_rows, cols), F32),
            V((out_rows, cols), F32),
            V((out_rows, width), BF16),
            sem((N_SEMS,)),
            sem((N_SEMS,)),
            sem((12,)),
            sem((4,)),
        ],
        compiler_params=pltpu.CompilerParams(
            collective_id=0, has_side_effects=True, vmem_limit_bytes=63 * 2**20
        ),
        name="window",
    )(
        pseudo_grads, master_slab, momentum, inner_inputs, token_ids.reshape(1, tokens),
        inner_weight, readout.reshape(4, g),
    )


def solution(mesh):
    in_specs = (
        P("island", "fsdp", None),
        P("fsdp", "island"),
        P("fsdp", "island"),
        P(("island", "fsdp"), None),
        P(("island", "fsdp")),
        P("island", "fsdp", None),
        P(),
    )
    out_specs = (
        P("fsdp", None),
        P("fsdp", "island"),
        P("fsdp", "island"),
        P("island", "fsdp", None),
        P(("island", "fsdp"), None),
    )
    return jax.shard_map(
        on_device, mesh=mesh, in_specs=in_specs, out_specs=out_specs, check_vma=False
    )
```

time: 375 us -> 149 us (0.40)
  waiting for transfers between devices: 305 us -> 0 us
  Pallas kernels: 0 us -> 139 us
  blocking collectives: 25.9 us -> 0 us
  matrix products: 23.5 us -> 0 us
  between operations: 15.5 us -> 0.65 us
  local copies, waits for them, and re-layouts: 1.82 us -> 9.69 us
    reduce_scatter x2 -> x0, waiting for transfers between devices: 176 us -> none  [the longest x1 176 us: inner_pass(): lax.psum_scatter(jnp.einsum('tf,tk->fk', slopes, inner_inputs, preferred_...]
    pallas_call x0 -> x1, Pallas kernels: none -> 139 us  [on_device(): pl.pallas_call(body, out_shape=(jax.ShapeDtypeStruct((out_rows, width), B...]
    all_gather x1 -> x0, waiting for transfers between devices: 127 us -> none  [inner_pass(): rows = lax.all_gather(weight, 'fsdp', axis=0, tiled=True)]
    all_gather x1 -> x0, blocking collectives: 25.9 us -> none  [outer_update(): new_slab = lax.all_gather(owned, 'island', axis=1, tiled=True)]
    dot_general x3 -> x0, matrix products: 23.5 us -> none  [the longest x1 8.3 us: inner_pass(): jnp.einsum('tf,tk->fk', slopes, inner_inputs, preferred_element_type=jnp....]
    unnamed x9 -> x7, local copies, waits for them, and re-layouts: 1.82 us -> 9.69 us
  transfers between devices with their start and end apart: 3 -> 0, of which waited for: 2 -> 0; matrix products, arithmetic and copies ran while one was open for 7% -> 0% of each run, Pallas kernels for 0% -> 0%
where the time goes in v1:
time: 149 us
  Pallas kernels  139 us (93%)
  local copies, waits for them, and re-layouts  9.69 us (7%)
    pallas_call x1, Pallas kernels, on_device(): pl.pallas_call(body, out_shape=(jax.ShapeDtypeStruct((out_rows, width), B...  139 us
    unnamed x7, local copies, waits for them, and re-layouts  9.69 us

profile of v1, /device:TPU:22, one launch (start us, length us, event | category | flops | bytes accessed | tf_op | source)
XLA Modules:
  0.0 149.1 jit_solution(18227700037961913037)
XLA Ops:
  0.6 138.8 %window.1 = (bf16[16,28672]{1,0:T(8,128)(2,1)}, f32[16,1792]{1,0:T(8,128)}, f32[16,1792]{1,0:T(8,128)}, f32[1,32,8192]{2,1,0:T(8,128)}, bf16[256,8192]{1,0:T(8,128)(2,1)}) custom-call(f32[1,16,28672]{2,1,0:T(8,128)} %refs_0_.1, f32[16,1792]{1,0:T(8,128)} %refs_1_.1, f32[16,1792]{1,0:T(8,128)} %refs_2_.1, bf16[256,8192]{1,0:T(8,128)(2,1)} %refs_3_.1, ...), custom_call_target="tpu_custom_call" | custom-call | tf_op jit(solution)/shard_map/window/pallas_call | solution.py:369
  139.4 0.0 copy-start
  139.4 2.3 %copy.17 = bf16[16,28672]{1,0:T(8,128)(2,1)} copy(bf16[16,28672]{1,0:T(8,128)(2,1)} %get-tuple-element.10) | data formatting | bytes 1835008
  141.7 1.6 %copy.18 = f32[16,1792]{1,0:T(8,128)} copy(f32[16,1792]{1,0:T(8,128)} %get-tuple-element.11) | data formatting | bytes 229376
  143.3 1.6 %copy.19 = f32[16,1792]{1,0:T(8,128)} copy(f32[16,1792]{1,0:T(8,128)} %get-tuple-element.12) | data formatting | bytes 229376
  144.8 2.3 %copy.20 = f32[1,32,8192]{2,1,0:T(8,128)} copy(f32[1,32,8192]{2,1,0:T(8,128)} %get-tuple-element.13) | data formatting | bytes 2097152
  147.1 0.0 copy-done
  147.1 2.0 %copy.21 = bf16[256,8192]{1,0:T(8,128)(2,1)} copy(bf16[256,8192]{1,0:T(8,128)(2,1)S(1)} %copy-done) | data formatting | bytes 8388608
Async XLA Ops:
  139.4 7.7 %copy-start = (bf16[256,8192]{1,0:T(8,128)(2,1)S(1)}, bf16[256,8192]{1,0:T(8,128)(2,1)}, u32[]{:S(2)}) copy-start(bf16[256,8192]{1,0:T(8,128)(2,1)} %get-tuple-element.14) | copy-start | bytes 12582916

commit v2 on v1

--- a/solution.py
+++ b/solution.py
@@ -15,10 +15,10 @@
 def kernel(
     groups, share, scale,
     pg, master, momentum, xin, tok, w, readout,
-    slab_out, master_out, momentum_out, wg_out, dx_out,
-    xb, wv, dwp, snd, slt, sl, dxb, tokb, rob, pre,
+    slab, master_out, momentum_out, wg_out, dxb,
+    xb, wv, dwp, snd, slt, sl, tokb, rob, pre,
     ra1, ra0, rt1, rt0, ru1, ru0, rv1, rv0,
-    acc, rc, rx, rz, msb, mob, slab,
+    acc, rc, rx, rz, msb, mob,
     ssem, rsem, lsem, gsem,
 ):
     f, i = lax.axis_index("fsdp"), lax.axis_index("island")
@@ -151,15 +151,17 @@
         dw(dh, 0, ka, ka // 5)
         dw(dh, ka, kb, kb)
 
-    def add(at_rows, lo, n, terms, step, keep=False, out=True):
+    def add(at_rows, lo, n, terms, step, keep=False, out=True, last=False):
         def body(j, carry):
             at = pl.ds(pl.multiple_of(lo + j * step, 128), step)
             total = dwp[at_rows, at]
             for ref, off in terms:
                 total = total + ref[:, pl.ds(pl.multiple_of(lo - off + j * step, 128), step)].astype(F32)
-            if keep:
+            if last:
+                wg_out[0, :, at] = total
+            elif keep:
                 dwp[at_rows, at] = total
-            if out:
+            if out and not last:
                 snd[at_rows, at] = total.astype(BF16)
             return carry
 
@@ -217,13 +219,12 @@
     lms.wait()
     lmo.wait()
     mean = (acc[x * 2 + z] + rz[...]) / groups
-    mob[...] = 0.9 * mob[...] + mean
-    msb[...] = msb[...] - 0.7 * (mean + 0.9 * mob[...])
+    stepped = 0.9 * mob[...] + mean
+    momentum_out[...] = stepped
+    master_out[...] = msb[...] - 0.7 * (mean + 0.9 * stepped)
     mine = block(i)
-    slab[:, mine] = msb[...].astype(BF16)
+    slab[:, mine] = master_out[...].astype(BF16)
     send("SZ", slab.at[:, mine], slab.at[:, mine], at_z)
-    load(msb, master_out, 7)
-    load(mob, momentum_out, 8)
 
     got("Ay+1", "Ay-1")
     send("Ayf+1", wv.at[rows(1, 3), A1], wv.at[rows(1, 3), A1], at_y(1))
@@ -296,7 +297,6 @@
         return carry
 
     lax.fori_loop(0, k // 512, dx, 0)
-    load(dxb, dx_out, 9)
     s3(2)
     s3(1)
     s3(3)
@@ -308,7 +308,6 @@
     send("U3+", snd.at[group(1), B1], ru0.at[0, :, pl.ds(0, hb)], at_h(1))
     send("U3-", snd.at[group(3), B2], ru0.at[1, :, pl.ds(hb, hb)], at_h(3))
     all_blocks(2, slab.at[:, pl.ds(0, slab.shape[1] // 2)]).wait_recv()
-    load(slab, slab_out, 10)
     sum_a(2)
     send("T1+", snd.at[rows(2, 0), A1], rt1.at[0], at_h(1))
     send("T1-", snd.at[rows(2, 0), A2], rt1.at[1], at_h(3))
@@ -335,17 +334,23 @@
     send("V3-", snd.at[rows(0, 3), B2], rv0.at[1, :, pl.ds(hb, hb)], at_y(3))
     sum_a(0)
     got("V2+", "V2-", "V3+", "V3-")
-    add(own, ka, kb, [(rv0.at[0], ka), (rv0.at[1], ka)], sb, keep=True, out=False)
+    add(own, ka, kb, [(rv0.at[0], ka), (rv0.at[1], ka)], sb, last=True)
     got("T2+", "T2-", "T3+", "T3-")
-    add(own, 0, ka, [(rt0.at[0], 0), (rt0.at[1], 0)], sa, keep=True, out=False)
-    load(dwp.at[own], wg_out.at[0], 11)
+    add(own, 0, ka, [(rt0.at[0], 0), (rt0.at[1], 0)], sa, last=True)
 
     for copy in copies.values():
         copy.wait_send()
     all_blocks(0, rc).wait_send()
     all_blocks(2, slab.at[:, pl.ds(0, slab.shape[1] // 2)]).wait_send()
-    for cp in loads[6:]:
-        cp.wait()
+
+
+def drain(*refs):
+    sems = refs[-1]
+    moves = [pltpu.make_async_copy(refs[n], refs[5 + n], sems.at[n]) for n in range(5)]
+    for move in moves:
+        move.start()
+    for move in moves:
+        move.wait()
 
 
 def on_device(pseudo_grads, master_slab, momentum, inner_inputs, token_ids, inner_weight, readout):
@@ -366,17 +371,18 @@
     def body(*refs):
         kernel(groups, share, scale, *refs)
 
-    return pl.pallas_call(
+    shapes = (
+        ((out_rows, width), BF16),
+        (master_slab.shape, F32),
+        (momentum.shape, F32),
+        ((1, r, k), F32),
+        ((tokens, k), BF16),
+    )
+    results = pl.pallas_call(
         body,
-        out_shape=(
-            jax.ShapeDtypeStruct((out_rows, width), BF16),
-            jax.ShapeDtypeStruct(master_slab.shape, F32),
-            jax.ShapeDtypeStruct(momentum.shape, F32),
-            jax.ShapeDtypeStruct((1, r, k), F32),
-            jax.ShapeDtypeStruct((tokens, k), BF16),
-        ),
+        out_shape=tuple(V(*shape) for shape in shapes),
         in_specs=[anywhere] * 7,
-        out_specs=[anywhere] * 5,
+        out_specs=[pl.BlockSpec(memory_space=pltpu.VMEM)] * 5,
         scratch_shapes=[
             V((tokens, k), BF16),
             V((features, k), BF16),
@@ -384,7 +390,6 @@
             V((features, k), BF16),
             V((features, tokens), BF16),
             V((tokens, features), BF16),
-            V((tokens, k), BF16),
             V((1, tokens), jnp.int32),
             V((4, g), F32),
             V((features, tokens), F32),
@@ -402,20 +407,28 @@
             V((out_rows, cols), F32),
             V((out_rows, cols), F32),
             V((out_rows, cols), F32),
-            V((out_rows, width), BF16),
             sem((N_SEMS,)),
             sem((N_SEMS,)),
             sem((12,)),
             sem((4,)),
         ],
         compiler_params=pltpu.CompilerParams(
-            collective_id=0, has_side_effects=True, vmem_limit_bytes=63 * 2**20
+            collective_id=0, has_side_effects=True, vmem_limit_bytes=54 * 2**20
         ),
         name="window",
     )(
         pseudo_grads, master_slab, momentum, inner_inputs, token_ids.reshape(1, tokens),
         inner_weight, readout.reshape(4, g),
     )
+    return pl.pallas_call(
+        drain,
+        out_shape=tuple(jax.ShapeDtypeStruct(*shape) for shape in shapes),
+        in_specs=[pl.BlockSpec(memory_space=pltpu.VMEM)] * 5,
+        out_specs=[anywhere] * 5,
+        scratch_shapes=[sem((5,))],
+        compiler_params=pltpu.CompilerParams(vmem_limit_bytes=2**20),
+        name="drain",
+    )(*(pltpu.with_memory_space_constraint(result, pltpu.VMEM) for result in results))
 
 
 def solution(mesh):

time: 149 us -> 141 us (0.946)
  local copies, waits for them, and re-layouts: 9.69 us -> 0 us
  Pallas kernels: 139 us -> 141 us
    unnamed x7 -> x0, local copies, waits for them, and re-layouts: 9.69 us -> none
    pallas_call x1 -> x2, Pallas kernels: 139 us -> 141 us  [the longest x1 138 us: on_device(): pl.pallas_call(body, out_shape=tuple((V(*shape) for shape in shapes)), in...]
where the time goes in v2:
time: 141 us
  Pallas kernels  141 us (100%)
    pallas_call x1, Pallas kernels, on_device(): pl.pallas_call(body, out_shape=tuple((V(*shape) for shape in shapes)), in...  138 us

profile of v2, /device:TPU:22, one launch (start us, length us, event | category | flops | bytes accessed | tf_op | source)
XLA Modules:
  0.0 141.3 jit_solution(7872214964285364028)
XLA Ops:
  0.6 137.9 %window.1 = (bf16[16,28672]{1,0:T(8,128)(2,1)S(1)}, f32[16,1792]{1,0:T(8,128)S(1)}, f32[16,1792]{1,0:T(8,128)S(1)}, f32[1,32,8192]{2,1,0:T(8,128)S(1)}, bf16[256,8192]{1,0:T(8,128)(2,1)S(1)}) custom-call(f32[1,16,28672]{2,1,0:T(8,128)} %refs_0_.1, f32[16,1792]{1,0:T(8,128)} %refs_1_.1, f32[16,1792]{1,0:T(8,128)} %refs_2_.1, bf16[256,8192]{1,0:T(8,128)(2,1)} %refs_3_.1, ...), custom_call_target="tpu_custom_call" | custom-call | tf_op jit(solution)/shard_map/window/pallas_call | solution.py:381
  138.6 2.8 %drain.1 = (bf16[16,28672]{1,0:T(8,128)(2,1)}, f32[16,1792]{1,0:T(8,128)}, f32[16,1792]{1,0:T(8,128)}, f32[1,32,8192]{2,1,0:T(8,128)}, bf16[256,8192]{1,0:T(8,128)(2,1)}) custom-call(bf16[16,28672]{1,0:T(8,128)(2,1)S(1)} %get-tuple-element.10.refs_0_, f32[16,1792]{1,0:T(8,128)S(1)} %get-tuple-element.11.refs_1_, f32[16,1792]{1,0:T(8,128)S(1)} %get-tuple-element.12.refs_2_, ...), custom_call_target="tpu_custom_call" | custom-call | tf_op jit(solution)/shard_map/drain/pallas_call | solution.py:423

commit v3 on v0

v3 whole, which is shorter than its diff:
```python
import math

import jax
import jax.numpy as jnp
from jax import lax
from jax.experimental import pallas as pl
from jax.experimental.pallas import tpu as pltpu
from jax.sharding import PartitionSpec as P

MESH = pl.DeviceIdType.MESH
F32, BF16 = jnp.float32, jnp.bfloat16
N_SEMS = 144


def kernel(
    groups, share, back_share, scale,
    pg, master, momentum, xin, tok, w, readout,
    slab, master_out, momentum_out, wg_out, dxb,
    xo, xp, wv, dwp, snd, slt, slo, spt, sp, dxs, tokb, rob, preo, ps, pr,
    ra, rt1, rt0, ru1, ru0, rb, rs,
    acc, rc, rx, rz, msb, mob,
    ssem, rsem, lsem, gsem,
):
    f, i = lax.axis_index("fsdp"), lax.axis_index("island")
    h, y = f // 4, lax.rem(f, 4)
    x, z, c = i // 4, lax.rem(i // 2, 2), lax.rem(i, 2)

    mate = (y + 1 - 2 * lax.rem(y, 2), 3 - y)
    far = 3 - mate[0]
    n = xo.shape[1] // 2
    side = (lax.rem((y + 1) // 2, 2), y // 2)
    base = tuple(2 * n * q + n * side[q] for q in range(2))
    mate_base = tuple(2 * n * q + n * (1 - side[q]) for q in range(2))

    def at_y(d):
        return {"fsdp": h * 4 + d}

    def at_h(d):
        return {"fsdp": lax.rem(h + d, 4) * 4 + y}

    def at_x(d):
        return {"island": lax.rem(x + d, 4) * 4 + z * 2 + c}

    at_z = {"island": x * 4 + (1 - z) * 2 + c}
    at_c = {"island": x * 4 + z * 2 + 1 - c}
    pair = tuple(at_y(mate[q]) for q in range(2))
    link = (pair[1], pair[0])
    ways = (("+", at_h(1), 3, 1), ("-", at_h(3), 1, 3))

    r = w.shape[1]
    g = r * 4
    half = g // 2
    full = tuple(pl.ds(q * n, n) for q in range(2))
    ca, cb = share, n - share
    A = (pl.ds(0, ca), pl.ds(n + cb, ca))
    B = (pl.ds(ca, cb), pl.ds(n, cb))
    BB = pl.ds(ca, 2 * cb)
    sa, sb = back_share, n - back_share
    a_lo, b_lo = (0, n + sb), (sa, n)
    SA = (pl.ds(0, sa), pl.ds(n + sb, sa))
    SB = (pl.ds(sa, sb), pl.ds(n, sb))
    SBB = pl.ds(sa, 2 * sb)

    def rows(dh, at):
        return pl.ds(pl.multiple_of(dh * g + at * r, r), r)

    def group(dh):
        return pl.ds(dh * g, g)

    def low(dh):
        return pl.ds(dh * g, half)

    def high(dh):
        return pl.ds(dh * g + half, half)

    def wide(start, size):
        return pl.ds(pl.multiple_of(start, 128), size)

    def own_w(q, lo, size):
        return w.at[0, :, wide(base[q] + lo - q * n, size)]

    copies = {}

    def send(name, src, dst, device):
        k = len(copies)
        copies[name] = pltpu.make_async_remote_copy(
            src_ref=src, dst_ref=dst, send_sem=ssem.at[k], recv_sem=rsem.at[k],
            device_id=device, device_id_type=MESH,
        )
        copies[name].start()

    def got(*names):
        for name in names:
            copies[name].wait_recv()

    def got_both(*names):
        for name in names:
            got(name + "0", name + "1")

    def got_ways(*names):
        for name in names:
            got(name + "+", name + "-")

    def load(src, dst, k):
        cp = pltpu.make_async_copy(src, dst, lsem.at[k])
        cp.start()
        return cp

    cols = slab.shape[1] // groups

    def block(k):
        return wide(k * cols, cols)

    mine_rows = rows(0, y)
    lw = [load(own_w(q, q * n, n), wv.at[mine_rows, full[q]], q) for q in range(2)]
    lx = [load(xin.at[:, wide(base[q], n)], xo.at[:, full[q]], 2 + q) for q in range(2)]
    small = [load(tok, tokb, 4), load(readout, rob, 5)]
    states = [load(master, msb, 6), load(momentum, mob, 7)]
    for j in range(8):
        pltpu.make_async_copy(pg.at[0, :, block(2 * j + c)], acc.at[j], lsem.at[8]).start()

    barrier = pltpu.get_barrier_semaphore()
    partners = [pair[0], pair[1], at_h(1), at_h(3), at_x(1), at_x(2), at_x(3), at_z, at_c]
    for device in partners:
        pl.semaphore_signal(barrier, inc=1, device_id=device, device_id_type=MESH)
    pl.semaphore_wait(barrier, len(partners))

    for q in range(2):
        send(f"w{q}", w.at[0, :, wide(mate_base[q], n)], wv.at[mine_rows, full[q]], pair[q])
    for q in range(2):
        for s, device, slot, _ in ways:
            send(f"wa{q}o{s}", own_w(q, A[q].start, ca), wv.at[rows(slot, y), A[q]], device)
    for q in range(2):
        send(f"ybo{q}", own_w(q, B[q].start, cb), wv.at[mine_rows, B[q]], link[q])
        send(f"ya0o{q}", own_w(q, A[q].start, ca), wv.at[mine_rows, A[q]], link[q])
    for j in range(8):
        pltpu.make_async_remote_copy(
            src_ref=pg.at[0, :, block(2 * j + 1 - c)], dst_ref=rc.at[j], send_sem=gsem.at[0], recv_sem=gsem.at[1],
            device_id=at_c, device_id_type=MESH,
        ).start()

    def all_blocks(k, ref):
        return pltpu.make_async_remote_copy(
            src_ref=ref, dst_ref=ref, send_sem=gsem.at[k], recv_sem=gsem.at[k + 1], device_id=at_c, device_id_type=MESH
        )

    def product(at_rows, xs, lo, size):
        def body(j, total):
            at = wide(lo + j * (n // 2), n // 2)
            return total + lax.dot_general(
                wv[at_rows, at], xs[:, at], (((1,), (1,)), ((), ())), preferred_element_type=F32
            )

        return lax.fori_loop(0, size // (n // 2), body, jnp.zeros((g, xs.shape[0]), F32))

    def pre(d):
        for q in range(2):
            ps[q, group(d)] = product(group(d), xp, q * n, n)
            send(f"p{d}{q}", ps.at[q, group(d)], pr.at[q, group(d)], pair[q])
        preo[group(d)] = product(group(d), xo, 0, 2 * n)

    def slope(d):
        got_both(f"p{d}")
        p = preo[group(d)] + pr[0, group(d)] + pr[1, group(d)]
        sig = jax.nn.sigmoid(p)
        keep = (tokb[...] != 0).astype(F32)
        row = rob[pl.ds(lax.rem(h + d, 4), 1), :]
        column = jnp.transpose(jnp.broadcast_to(row, (g, g)))
        weight = jnp.concatenate([column] * (p.shape[1] // g), axis=1)
        value = scale * keep * weight * (sig * (1.0 + p * (1.0 - sig)))
        slt[group(d)] = value.astype(BF16)
        for q in range(2):
            send(f"s{d}{q}", slt.at[group(d)], spt.at[q, group(d)], pair[q])
        slo[:, group(d)] = jnp.transpose(value).astype(BF16)

    def dw(d):
        got_both(f"s{d}")
        own = slt[group(d)]
        for q in range(2):
            other = spt[q, group(d)]

            def body(j, carry, q=q, other=other):
                at = wide(q * n + j * (n // 2), n // 2)
                part = jnp.dot(own, xo[:, at], preferred_element_type=F32) + jnp.dot(
                    other, xp[:, at], preferred_element_type=F32
                )
                dwp[group(d), at] = part
                snd[group(d), at] = part.astype(BF16)
                return carry

            lax.fori_loop(0, 2, body, 0)

    def turn(d):
        for q in range(2):
            sp[q, :, group(d)] = jnp.transpose(spt[q, group(d)].astype(F32)).astype(BF16)

    def add(at_rows, lo, size, terms, to=None):
        units = size // 128
        step = 128 * max(k for k in range(1, 6) if units % k == 0)

        def body(j, carry):
            at = wide(lo + j * step, step)
            there = wide(j * step, step)
            total = dwp[at_rows, at]
            for ref in terms:
                total = total + ref[:, there].astype(F32)
            if to != "snd":
                dwp[at_rows, at] = total
            if to != "dwp":
                snd[at_rows, at] = total.astype(BF16)
            return carry

        lax.fori_loop(0, size // step, body, 0)

    def across(d, at):
        for q in range(2):
            part = wv.at[rows(d, y if at == "o" else mate[q]), A[q]]
            send(f"ya{d}{at}{q}", part, part, link[q])

    got_both("w")
    for q in range(2):
        part = wv.at[rows(0, mate[q]), B[q]]
        send(f"ybm{q}", part, part, link[q])
    across(0, "m")
    for q in range(2):
        for s, device, slot, _ in ways:
            send(f"wa{q}m{s}", wv.at[rows(0, mate[q]), A[q]], wv.at[rows(slot, mate[q]), A[q]], device)
    for q in range(2):
        send(f"x{q}", xin.at[:, wide(mate_base[q], n)], xp.at[:, full[q]], pair[q])
    got_both("ybo", "ybm")
    lw[0].wait()
    lw[1].wait()
    for s, device, slot, _ in ways:
        send(f"hb{s}", wv.at[group(0), BB], wv.at[group(slot), BB], device)
    got_ways("wa0o", "wa1o")
    for q in range(2):
        send(f"wf{q}+", wv.at[rows(3, y), A[q]], wv.at[rows(2, y), A[q]], at_h(1))
    across(3, "o")
    across(1, "o")
    got_ways("wa0m", "wa1m")
    for q in range(2):
        send(f"wf{q}-", wv.at[rows(1, mate[q]), A[q]], wv.at[rows(2, mate[q]), A[q]], at_h(3))
    across(3, "m")
    across(1, "m")

    pltpu.make_async_copy(acc, acc, lsem.at[8]).wait()
    all_blocks(0, rc).wait_recv()
    for j in range(8):
        acc[j] = acc[j] + rc[j]
    for d in (1, 3, 2):
        send(f"X{d}", acc.at[pl.ds(lax.rem(x + d, 4) * 2, 2)], rx.at[d - 1], at_x(d))
    got("X1", "X3", "X2")
    two = acc.at[pl.ds(x * 2, 2)]
    two[...] = two[...] + rx[0] + rx[1] + rx[2]
    send("Z", acc.at[x * 2 + 1 - z], rz, at_z)

    for cp in lx + small + states:
        cp.wait()
    got_both("ya0o", "ya0m", "x")
    pre(0)
    got_ways("hb")
    send("hbf+", wv.at[low(3), BB], wv.at[low(2), BB], at_h(1))
    send("hbf-", wv.at[high(1), BB], wv.at[high(2), BB], at_h(3))
    got_both("ya3o", "ya3m")
    pre(3)
    got_ways("wf0", "wf1")
    across(2, "o")
    across(2, "m")
    got_both("ya1o", "ya1m")
    pre(1)
    slope(0)

    got("Z")
    mean = (acc[x * 2 + z] + rz[...]) / groups
    stepped = 0.9 * mob[...] + mean
    momentum_out[...] = stepped
    master_out[...] = msb[...] - 0.7 * (mean + 0.9 * stepped)
    mine = block(i)
    slab[:, mine] = master_out[...].astype(BF16)
    send("SZ", slab.at[:, mine], slab.at[:, mine], at_z)

    slope(3)
    slope(1)
    got_both("ya2o", "ya2m")
    got_ways("hbf")
    pre(2)
    dw(0)
    dw(3)
    dw(1)

    def across_back(d):
        for q in range(2):
            for k, at in enumerate((mate[1 - q], far)):
                send(f"sa{d}{k}{q}", snd.at[rows(d, at), SA[q]], ra.at[q, d, k], link[q])

    def sum_across(d, to=None):
        got_both(f"sa{d}0", f"sa{d}1")
        for q in range(2):
            add(rows(d, y), a_lo[q], sa, [ra.at[q, d, 0]], to)
            add(rows(d, mate[q]), a_lo[q], sa, [ra.at[q, d, 1]], to)

    send("U2+", snd.at[high(1), SBB], ru0.at[0, pl.ds(half, half)], at_h(1))
    send("U2-", snd.at[low(3), SBB], ru0.at[1, pl.ds(0, half)], at_h(3))
    across_back(1)
    slope(2)
    across_back(3)
    got("SZ")
    other = block(x * 4 + (1 - z) * 2 + c)
    for d in (1, 3, 2):
        send(f"SX{d}", slab.at[:, mine], slab.at[:, mine], at_x(d))
        send(f"SY{d}", slab.at[:, other], slab.at[:, other], at_x(d))
    for d in (0, 3, 1):
        turn(d)
    dw(2)
    send("U1+", snd.at[low(2), SBB], ru1.at[0], at_h(1))
    send("U1-", snd.at[high(2), SBB], ru1.at[1], at_h(3))
    across_back(2)
    across_back(0)
    turn(2)

    def dx_mate(q):
        def body(j, carry):
            at = wide(q * n + j * (n // 4), n // 4)
            dxs[:, at] = jnp.dot(sp[q], wv[:, at], preferred_element_type=F32).astype(BF16)
            return carry

        lax.fori_loop(0, 4, body, 0)
        send(f"dx{q}", dxs.at[:, full[q]], dxb.at[:, wide(base[q], n)], pair[q])

    sum_across(1)
    for q in range(2):
        send(f"T2{q}+", snd.at[rows(1, mate[q]), SA[q]], rt0.at[q, 0, 1], at_h(1))
    dx_mate(0)
    sum_across(3)
    for q in range(2):
        send(f"T2{q}-", snd.at[rows(3, y), SA[q]], rt0.at[q, 1, 0], at_h(3))
    dx_mate(1)

    sum_across(2)
    for q in range(2):
        send(f"T1{q}+", snd.at[rows(2, y), SA[q]], rt1.at[q, 0], at_h(1))
        send(f"T1{q}-", snd.at[rows(2, mate[q]), SA[q]], rt1.at[q, 1], at_h(3))
    got_ways("U1")
    add(low(1), SBB.start, 2 * sb, [ru1.at[0]], "snd")
    add(high(3), SBB.start, 2 * sb, [ru1.at[1]], "snd")
    send("U3+", snd.at[low(1), SBB], ru0.at[0, pl.ds(0, half)], at_h(1))
    send("U3-", snd.at[high(3), SBB], ru0.at[1, pl.ds(half, half)], at_h(3))
    got("SX1", "SX3", "SX2", "SY1", "SY3", "SY2")
    for j in range(8):
        at = block(2 * j + c)
        pltpu.make_async_remote_copy(
            src_ref=slab.at[:, at], dst_ref=slab.at[:, at], send_sem=gsem.at[2], recv_sem=gsem.at[3],
            device_id=at_c, device_id_type=MESH,
        ).start()
    for q in range(2):
        got_ways(f"T1{q}")
        add(rows(1, y), a_lo[q], sa, [rt1.at[q, 0]], "snd")
        add(rows(3, mate[q]), a_lo[q], sa, [rt1.at[q, 1]], "snd")
        send(f"T3{q}+", snd.at[rows(1, y), SA[q]], rt0.at[q, 0, 0], at_h(1))
        send(f"T3{q}-", snd.at[rows(3, mate[q]), SA[q]], rt0.at[q, 1, 1], at_h(3))
    for q in range(2):

        def dx_own(j, carry, q=q):
            at = wide(q * n + j * (n // 4), n // 4)
            there = wide(base[q] + j * (n // 4), n // 4)
            dxb[:, there] = jnp.dot(slo[...], wv[:, at], preferred_element_type=F32).astype(BF16)
            return carry

        lax.fori_loop(0, 4, dx_own, 0)
    sum_across(0, "dwp")
    got_ways("U2", "U3")
    add(group(0), SBB.start, 2 * sb, [ru0.at[0], ru0.at[1]])
    for q in range(2):
        for k, at in enumerate((mate[1 - q], far)):
            send(f"sb{k}{q}", snd.at[rows(0, at), SB[q]], rb.at[q, k], link[q])
    got_both("sb0", "sb1")
    for q in range(2):
        add(mine_rows, b_lo[q], sb, [rb.at[q, 0]], "dwp")
        add(rows(0, mate[q]), b_lo[q], sb, [rb.at[q, 1]], "snd")
        send(f"fb{q}", snd.at[rows(0, mate[q]), SB[q]], rs.at[q, :, pl.ds(b_lo[q] - q * n, sb)], pair[q])
    for q in range(2):
        got_ways(f"T2{q}", f"T3{q}")
        add(rows(0, mate[q]), a_lo[q], sa, [rt0.at[q, 0, 1], rt0.at[q, 1, 1]], "snd")
        send(f"fa{q}", snd.at[rows(0, mate[q]), SA[q]], rs.at[q, :, pl.ds(a_lo[q] - q * n, sa)], pair[q])
    for q in range(2):
        add(mine_rows, a_lo[q], sa, [rt0.at[q, 0, 0], rt0.at[q, 1, 0]], "dwp")
        wg_out[0, :, wide(base[q], n)] = dwp[mine_rows, full[q]]
    for q in range(2):
        got(f"fa{q}", f"fb{q}")
        wg_out[0, :, wide(mate_base[q], n)] = rs[q].astype(F32)
    got_both("dx")
    all_blocks(2, slab.at[:, pl.ds(0, slab.shape[1] // 2)]).wait_recv()

    for copy in copies.values():
        copy.wait_send()
    all_blocks(0, rc).wait_send()
    all_blocks(2, slab.at[:, pl.ds(0, slab.shape[1] // 2)]).wait_send()


def drain(*refs):
    sems = refs[-1]
    moves = [pltpu.make_async_copy(refs[n], refs[5 + n], sems.at[n]) for n in range(5)]
    for move in moves:
        move.start()
    for move in moves:
        move.wait()


def on_device(pseudo_grads, master_slab, momentum, inner_inputs, token_ids, inner_weight, readout):
    groups = lax.axis_size("island")
    tokens, k = inner_inputs.shape
    r = inner_weight.shape[1]
    features = readout.shape[0]
    g = 4 * r
    width, cols = pseudo_grads.shape[2], master_slab.shape[1]
    out_rows = pseudo_grads.shape[1]
    n = k // 4
    share, back_share = 9 * n // 16, 12 * n // 16
    sa, sb = back_share, n - back_share
    scale = 1.0 / math.sqrt(tokens * lax.axis_size("fsdp"))
    V, sem = pltpu.VMEM, pltpu.SemaphoreType.DMA
    anywhere = pl.BlockSpec(memory_space=pl.ANY)

    def body(*refs):
        kernel(groups, share, back_share, scale, *refs)

    shapes = (
        ((out_rows, width), BF16),
        (master_slab.shape, F32),
        (momentum.shape, F32),
        ((1, r, k), F32),
        ((tokens, k), BF16),
    )
    results = pl.pallas_call(
        body,
        out_shape=tuple(V(*shape) for shape in shapes),
        in_specs=[anywhere] * 7,
        out_specs=[pl.BlockSpec(memory_space=pltpu.VMEM)] * 5,
        scratch_shapes=[
            V((tokens, 2 * n), BF16),
            V((tokens, 2 * n), BF16),
            V((features, 2 * n), BF16),
            V((features, 2 * n), F32),
            V((features, 2 * n), BF16),
            V((features, tokens), BF16),
            V((tokens, features), BF16),
            V((2, features, tokens), BF16),
            V((2, tokens, features), BF16),
            V((tokens, 2 * n), BF16),
            V((1, tokens), jnp.int32),
            V((4, g), F32),
            V((features, tokens), F32),
            V((2, features, tokens), F32),
            V((2, features, tokens), F32),
            V((2, 4, 2, r, sa), BF16),
            V((2, 2, r, sa), BF16),
            V((2, 2, 2, r, sa), BF16),
            V((2, g // 2, 2 * sb), BF16),
            V((2, g, 2 * sb), BF16),
            V((2, 2, r, sb), BF16),
            V((2, r, n), BF16),
            V((8, out_rows, cols), F32),
            V((8, out_rows, cols), F32),
            V((3, 2, out_rows, cols), F32),
            V((out_rows, cols), F32),
            V((out_rows, cols), F32),
            V((out_rows, cols), F32),
            sem((N_SEMS,)),
            sem((N_SEMS,)),
            sem((12,)),
            sem((4,)),
        ],
        compiler_params=pltpu.CompilerParams(
            collective_id=0, has_side_effects=True, vmem_limit_bytes=54 * 2**20
        ),
        name="window",
    )(
        pseudo_grads, master_slab, momentum, inner_inputs, token_ids.reshape(1, tokens),
        inner_weight, readout.reshape(4, g),
    )
    return pl.pallas_call(
        drain,
        out_shape=tuple(jax.ShapeDtypeStruct(*shape) for shape in shapes),
        in_specs=[pl.BlockSpec(memory_space=pltpu.VMEM)] * 5,
        out_specs=[anywhere] * 5,
        scratch_shapes=[sem((5,))],
        compiler_params=pltpu.CompilerParams(vmem_limit_bytes=2**20),
        name="drain",
    )(*(pltpu.with_memory_space_constraint(result, pltpu.VMEM) for result in results))


def solution(mesh):
    in_specs = (
        P("island", "fsdp", None),
        P("fsdp", "island"),
        P("fsdp", "island"),
        P(("island", "fsdp"), None),
        P(("island", "fsdp")),
        P("island", "fsdp", None),
        P(),
    )
    out_specs = (
        P("fsdp", None),
        P("fsdp", "island"),
        P("fsdp", "island"),
        P("island", "fsdp", None),
        P(("island", "fsdp"), None),
    )
    return jax.shard_map(
        on_device, mesh=mesh, in_specs=in_specs, out_specs=out_specs, check_vma=False
    )
```

time: 375 us -> 125 us (0.33)
  waiting for transfers between devices: 305 us -> 0 us
  Pallas kernels: 0 us -> 122 us
  blocking collectives: 25.9 us -> 0 us
  matrix products: 23.5 us -> 0 us
  between operations: 15.5 us -> 0.64 us
    reduce_scatter x2 -> x0, waiting for transfers between devices: 176 us -> none  [the longest x1 176 us: inner_pass(): lax.psum_scatter(jnp.einsum('tf,tk->fk', slopes, inner_inputs, preferred_...]
    all_gather x1 -> x0, waiting for transfers between devices: 127 us -> none  [inner_pass(): rows = lax.all_gather(weight, 'fsdp', axis=0, tiled=True)]
    pallas_call x0 -> x2, Pallas kernels: none -> 122 us  [the longest x1 119 us: on_device(): pl.pallas_call(body, out_shape=tuple((V(*shape) for shape in shapes)), in...]
    all_gather x1 -> x0, blocking collectives: 25.9 us -> none  [outer_update(): new_slab = lax.all_gather(owned, 'island', axis=1, tiled=True)]
    dot_general x3 -> x0, matrix products: 23.5 us -> none  [the longest x1 8.3 us: inner_pass(): jnp.einsum('tf,tk->fk', slopes, inner_inputs, preferred_element_type=jnp....]
  transfers between devices with their start and end apart: 3 -> 0, of which waited for: 2 -> 0; matrix products, arithmetic and copies ran while one was open for 7% -> 0% of each run, Pallas kernels for 0% -> 0%
where the time goes in v3:
time: 125 us; the launch traced here: 123 us
  Pallas kernels  122 us (98%)
    pallas_call x1, Pallas kernels, on_device(): pl.pallas_call(body, out_shape=tuple((V(*shape) for shape in shapes)), in...  119 us
    pallas_call x1, Pallas kernels, on_device(): pl.pallas_call(drain, out_shape=tuple((jax.ShapeDtypeStruct(*shape) for s...  2.78 us

profile of v3, /device:TPU:22, one launch (start us, length us, event | category | flops | bytes accessed | tf_op | source)
XLA Modules:
  0.0 122.9 jit_solution(7858145121755201582)
XLA Ops:
  0.6 119.5 %window.1 = (bf16[16,28672]{1,0:T(8,128)(2,1)S(1)}, f32[16,1792]{1,0:T(8,128)S(1)}, f32[16,1792]{1,0:T(8,128)S(1)}, f32[1,32,8192]{2,1,0:T(8,128)S(1)}, bf16[256,8192]{1,0:T(8,128)(2,1)S(1)}) custom-call(f32[1,16,28672]{2,1,0:T(8,128)} %refs_0_.1, f32[16,1792]{1,0:T(8,128)} %refs_1_.1, f32[16,1792]{1,0:T(8,128)} %refs_2_.1, bf16[256,8192]{1,0:T(8,128)(2,1)} %refs_3_.1, ...), custom_call_target="tpu_custom_call" | custom-call | tf_op jit(solution)/shard_map/window/pallas_call | solution.py:434
  120.1 2.8 %drain.1 = (bf16[16,28672]{1,0:T(8,128)(2,1)}, f32[16,1792]{1,0:T(8,128)}, f32[16,1792]{1,0:T(8,128)}, f32[1,32,8192]{2,1,0:T(8,128)}, bf16[256,8192]{1,0:T(8,128)(2,1)}) custom-call(bf16[16,28672]{1,0:T(8,128)(2,1)S(1)} %get-tuple-element.10.refs_0_, f32[16,1792]{1,0:T(8,128)S(1)} %get-tuple-element.11.refs_1_, f32[16,1792]{1,0:T(8,128)S(1)} %get-tuple-element.12.refs_2_, ...), custom_call_target="tpu_custom_call" | custom-call | tf_op jit(solution)/shard_map/drain/pallas_call | solution.py:481

commit v4 on v3

v4 whole, which is shorter than its diff:
```python
import math

import jax
import jax.numpy as jnp
from jax import lax
from jax.experimental import pallas as pl
from jax.experimental.pallas import tpu as pltpu
from jax.sharding import PartitionSpec as P

MESH = pl.DeviceIdType.MESH
F32, BF16 = jnp.float32, jnp.bfloat16
N_SEMS = 96


def kernel(
    groups, share, back_share, scale,
    pg, master, momentum, xin, tok, w, readout,
    slab, master_out, momentum_out, wg_out, dxb,
    xo, xp, wv, dwp, snd, slt, slo, spt, sp, dxs, tokb, rob, preo, ps, pr,
    ra, rt1, rt0, ru1, ru0, rb, rs,
    acc, rc, rx, rz, msb, mob,
    ssem, rsem, lsem, gsem,
):
    f, i = lax.axis_index("fsdp"), lax.axis_index("island")
    h, y = f // 4, lax.rem(f, 4)
    x, z, c = i // 4, lax.rem(i // 2, 2), lax.rem(i, 2)

    one, two = y + 1 - 2 * lax.rem(y, 2), 3 - y
    mate = one + c * (two - one)
    near = two + c * (one - two)
    far = 3 - one
    n = xo.shape[1]
    side = lax.rem((y + 1) // 2, 2) * (1 - c) + (y // 2) * c
    base, mate_base = n * side, n * (1 - side)

    def at_y(d):
        return {"fsdp": h * 4 + d}

    def at_h(d):
        return {"fsdp": lax.rem(h + d, 4) * 4 + y}

    def at_x(d):
        return {"island": lax.rem(x + d, 4) * 4 + z * 2 + c}

    at_z = {"island": x * 4 + (1 - z) * 2 + c}
    at_c = {"island": x * 4 + z * 2 + 1 - c}
    pair, link = at_y(mate), at_y(near)
    ways = (("+", at_h(1), 3), ("-", at_h(3), 1))

    r = w.shape[1]
    g = r * 4
    half = g // 2
    ca, cb = share, n - share
    A, B = pl.ds(0, ca), pl.ds(ca, cb)
    sa, sb = back_share, n - back_share
    SA, SB = pl.ds(0, sa), pl.ds(sa, sb)

    def rows(dh, at):
        return pl.ds(pl.multiple_of(dh * g + at * r, r), r)

    def group(dh):
        return pl.ds(dh * g, g)

    def low(dh):
        return pl.ds(dh * g, half)

    def high(dh):
        return pl.ds(dh * g + half, half)

    def wide(start, size):
        return pl.ds(pl.multiple_of(start, 128), size)

    def own_w(lo, size):
        return w.at[0, :, wide(base + lo, size)]

    copies = {}

    def send(name, src, dst, device):
        k = len(copies)
        copies[name] = pltpu.make_async_remote_copy(
            src_ref=src, dst_ref=dst, send_sem=ssem.at[k], recv_sem=rsem.at[k],
            device_id=device, device_id_type=MESH,
        )
        copies[name].start()

    def got(*names):
        for name in names:
            copies[name].wait_recv()

    def got_ways(*names):
        for name in names:
            got(name + "+", name + "-")

    def load(src, dst, k):
        cp = pltpu.make_async_copy(src, dst, lsem.at[k])
        cp.start()
        return cp

    cols = slab.shape[1] // groups

    def block(k):
        return wide(k * cols, cols)

    mine_rows = rows(0, y)
    lw = load(own_w(0, n), wv.at[mine_rows], 0)
    lx = load(xin.at[:, wide(base, n)], xo, 1)
    small = [load(tok, tokb, 4), load(readout, rob, 5)]
    states = [load(master, msb, 6), load(momentum, mob, 7)]
    for j in range(8):
        pltpu.make_async_copy(pg.at[0, :, block(2 * j + c)], acc.at[j], lsem.at[8]).start()

    barrier = pltpu.get_barrier_semaphore()
    partners = [pair, link, at_h(1), at_h(3), at_x(1), at_x(2), at_x(3), at_z, at_c]
    for device in partners:
        pl.semaphore_signal(barrier, inc=1, device_id=device, device_id_type=MESH)
    pl.semaphore_wait(barrier, len(partners))

    send("w", w.at[0, :, wide(mate_base, n)], wv.at[mine_rows], pair)
    for s, device, slot in ways:
        send(f"wao{s}", own_w(0, ca), wv.at[rows(slot, y), A], device)
    send("ybo", own_w(ca, cb), wv.at[mine_rows, B], link)
    for j in range(8):
        pltpu.make_async_remote_copy(
            src_ref=pg.at[0, :, block(2 * j + 1 - c)], dst_ref=rc.at[j], send_sem=gsem.at[0], recv_sem=gsem.at[1],
            device_id=at_c, device_id_type=MESH,
        ).start()

    def all_blocks(k, ref):
        return pltpu.make_async_remote_copy(
            src_ref=ref, dst_ref=ref, send_sem=gsem.at[k], recv_sem=gsem.at[k + 1], device_id=at_c, device_id_type=MESH
        )

    def product(at_rows, xs):
        def body(j, total):
            at = wide(j * (n // 4), n // 4)
            return total + lax.dot_general(
                wv[at_rows, at], xs[:, at], (((1,), (1,)), ((), ())), preferred_element_type=F32
            )

        return lax.fori_loop(0, 4, body, jnp.zeros((g, xs.shape[0]), F32))

    def pre_mate(d):
        ps[group(d)] = product(group(d), xp)
        send(f"p{d}", ps.at[group(d)], pr.at[group(d)], pair)

    def pre_own(d):
        preo[group(d)] = product(group(d), xo)

    def slope(d):
        got(f"p{d}")
        p = preo[group(d)] + pr[group(d)]
        sig = jax.nn.sigmoid(p)
        keep = (tokb[...] != 0).astype(F32)
        row = rob[pl.ds(lax.rem(h + d, 4), 1), :]
        column = jnp.transpose(jnp.broadcast_to(row, (g, g)))
        weight = jnp.concatenate([column] * (p.shape[1] // g), axis=1)
        value = scale * keep * weight * (sig * (1.0 + p * (1.0 - sig)))
        slt[group(d)] = value.astype(BF16)
        send(f"s{d}", slt.at[group(d)], spt.at[group(d)], pair)
        slo[:, group(d)] = jnp.transpose(value).astype(BF16)

    def dw(d):
        got(f"s{d}")
        own, other = slt[group(d)], spt[group(d)]

        def body(j, carry):
            at = wide(j * (n // 4), n // 4)
            part = jnp.dot(own, xo[:, at], preferred_element_type=F32) + jnp.dot(
                other, xp[:, at], preferred_element_type=F32
            )
            dwp[group(d), at] = part
            snd[group(d), at] = part.astype(BF16)
            return carry

        lax.fori_loop(0, 4, body, 0)

    def add(at_rows, lo, size, terms, to=None):
        units = size // 128
        step = 128 * max(k for k in range(1, 13 if at_rows.size == r else 6) if units % k == 0)

        def body(j, carry):
            at = wide(lo + j * step, step)
            there = wide(j * step, step)
            total = dwp[at_rows, at]
            for ref in terms:
                total = total + ref[:, there].astype(F32)
            if to != "snd":
                dwp[at_rows, at] = total
            if to != "dwp":
                snd[at_rows, at] = total.astype(BF16)
            return carry

        lax.fori_loop(0, size // step, body, 0)

    def across(d, at):
        part = wv.at[rows(d, y if at == "o" else mate), A]
        send(f"ya{d}{at}", part, part, link)

    def across_done(d):
        got(f"ya{d}o", f"ya{d}m")

    def across_back(d):
        for k, at in enumerate((near, far)):
            send(f"sa{d}{k}", snd.at[rows(d, at), SA], ra.at[d, k], link)

    def sum_across(d, to=None):
        got(f"sa{d}0", f"sa{d}1")
        add(rows(d, y), 0, sa, [ra.at[d, 0]], to)
        add(rows(d, mate), 0, sa, [ra.at[d, 1]], to)

    def dx_mate(k):
        def body(j, carry):
            at = wide(k * (n // 2) + j * (n // 4), n // 4)
            dxs[:, at] = jnp.dot(sp[...], wv[:, at], preferred_element_type=F32).astype(BF16)
            return carry

        lax.fori_loop(0, 2, body, 0)
        at = pl.ds(k * (n // 2), n // 2)
        send(f"dx{k}", dxs.at[:, at], dxb.at[:, wide(base + k * (n // 2), n // 2)], pair)

    def dx_own():
        def body(j, carry):
            at = wide(j * (n // 4), n // 4)
            there = wide(base + j * (n // 4), n // 4)
            dxb[:, there] = jnp.dot(slo[...], wv[:, at], preferred_element_type=F32).astype(BF16)
            return carry

        lax.fori_loop(0, 4, body, 0)

    got("w")
    part = wv.at[rows(0, mate), B]
    send("ybm", part, part, link)
    for s, device, slot in ways:
        send(f"wam{s}", wv.at[rows(0, mate), A], wv.at[rows(slot, mate), A], device)
    send("x", xin.at[:, wide(mate_base, n)], xp, pair)
    got("ybo", "ybm")
    lw.wait()
    for s, device, slot in ways:
        send(f"hb{s}", wv.at[group(0), B], wv.at[group(slot), B], device)
    got_ways("wao")
    send("wf+", wv.at[rows(3, y), A], wv.at[rows(2, y), A], at_h(1))
    across(3, "o")
    across(1, "o")
    got_ways("wam")
    send("wf-", wv.at[rows(1, mate), A], wv.at[rows(2, mate), A], at_h(3))
    across(3, "m")
    across(1, "m")

    pltpu.make_async_copy(acc, acc, lsem.at[8]).wait()
    all_blocks(0, rc).wait_recv()
    for j in range(8):
        acc[j] = acc[j] + rc[j]
    for d in (1, 3, 2):
        send(f"X{d}", acc.at[pl.ds(lax.rem(x + d, 4) * 2, 2)], rx.at[d - 1], at_x(d))
    got("X1", "X3", "X2")
    blocks = acc.at[pl.ds(x * 2, 2)]
    blocks[...] = blocks[...] + rx[0] + rx[1] + rx[2]

    lx.wait()
    for cp in small + states:
        cp.wait()
    got_ways("hb")
    send("hbf+", wv.at[low(3), B], wv.at[low(2), B], at_h(1))
    send("hbf-", wv.at[high(1), B], wv.at[high(2), B], at_h(3))
    send("Z", acc.at[x * 2 + 1 - z], rz, at_z)
    across_done(3)
    across_done(1)
    pre_own(3)
    got("x")
    pre_mate(3)
    pre_mate(1)
    got_ways("wf")
    pre_own(1)
    across(2, "m")
    across(2, "o")
    across(0, "m")
    slope(3)
    across(0, "o")
    slope(1)
    dw(3)
    dw(1)
    got_ways("hbf")
    send("U2+", snd.at[high(1), SB], ru0.at[0, pl.ds(half, half)], at_h(1))
    send("U2-", snd.at[low(3), SB], ru0.at[1, pl.ds(0, half)], at_h(3))
    across_done(2)
    pre_mate(2)
    pre_own(2)

    got("Z")
    mean = (acc[x * 2 + z] + rz[...]) / groups
    stepped = 0.9 * mob[...] + mean
    momentum_out[...] = stepped
    master_out[...] = msb[...] - 0.7 * (mean + 0.9 * stepped)
    mine = block(i)
    slab[:, mine] = master_out[...].astype(BF16)
    send("SZ", slab.at[:, mine], slab.at[:, mine], at_z)

    slope(2)
    across_done(0)
    pre_mate(0)
    across_back(1)
    dw(2)
    send("U1+", snd.at[low(2), SB], ru1.at[0], at_h(1))
    send("U1-", snd.at[high(2), SB], ru1.at[1], at_h(3))
    across_back(2)
    across_back(3)
    pre_own(0)
    slope(0)
    dw(0)
    across_back(0)
    sum_across(2)
    send("T1+", snd.at[rows(2, y), SA], rt1.at[0], at_h(1))
    send("T1-", snd.at[rows(2, mate), SA], rt1.at[1], at_h(3))

    got("SZ")
    other = block(x * 4 + (1 - z) * 2 + c)
    for d in (1, 3, 2):
        send(f"SX{d}", slab.at[:, mine], slab.at[:, mine], at_x(d))
        send(f"SY{d}", slab.at[:, other], slab.at[:, other], at_x(d))

    sum_across(3)
    sum_across(1)
    for d in range(4):
        sp[:, group(d)] = jnp.transpose(spt[group(d)].astype(F32)).astype(BF16)
    dx_mate(1)
    got_ways("U1")
    add(low(1), sa, sb, [ru1.at[0]], "snd")
    add(high(3), sa, sb, [ru1.at[1]], "snd")
    send("U3+", snd.at[low(1), SB], ru0.at[0, pl.ds(0, half)], at_h(1))
    send("U3-", snd.at[high(3), SB], ru0.at[1, pl.ds(half, half)], at_h(3))
    dx_mate(0)
    got_ways("T1")
    add(rows(1, y), 0, sa, [rt1.at[0]], "snd")
    add(rows(3, mate), 0, sa, [rt1.at[1]], "snd")
    send("T3+", snd.at[rows(1, y), SA], rt0.at[0, 0], at_h(1))
    send("T3-", snd.at[rows(3, mate), SA], rt0.at[1, 1], at_h(3))
    send("T2+", snd.at[rows(1, mate), SA], rt0.at[0, 1], at_h(1))
    send("T2-", snd.at[rows(3, y), SA], rt0.at[1, 0], at_h(3))
    sum_across(0, "dwp")
    dx_own()

    got("SX1", "SX3", "SX2", "SY1", "SY3", "SY2")
    for j in range(8):
        at = block(2 * j + c)
        pltpu.make_async_remote_copy(
            src_ref=slab.at[:, at], dst_ref=slab.at[:, at], send_sem=gsem.at[2], recv_sem=gsem.at[3],
            device_id=at_c, device_id_type=MESH,
        ).start()

    got_ways("U2", "U3")
    add(group(0), sa, sb, [ru0.at[0], ru0.at[1]])
    for k, at in enumerate((near, far)):
        send(f"sb{k}", snd.at[rows(0, at), SB], rb.at[k], link)
    got("sb0", "sb1")
    add(rows(0, mate), sa, sb, [rb.at[1]], "snd")
    send("fb", snd.at[rows(0, mate), SB], rs.at[:, SB], pair)
    add(mine_rows, sa, sb, [rb.at[0]], "dwp")
    got_ways("T2", "T3")
    add(rows(0, mate), 0, sa, [rt0.at[0, 1], rt0.at[1, 1]], "snd")
    send("fa", snd.at[rows(0, mate), SA], rs.at[:, SA], pair)
    add(mine_rows, 0, sa, [rt0.at[0, 0], rt0.at[1, 0]], "dwp")
    wg_out[0, :, wide(base, n)] = dwp[mine_rows, :]
    got("fa", "fb")
    wg_out[0, :, wide(mate_base, n)] = rs[...].astype(F32)
    got("dx0", "dx1")
    all_blocks(2, slab.at[:, pl.ds(0, slab.shape[1] // 2)]).wait_recv()

    for copy in copies.values():
        copy.wait_send()
    all_blocks(0, rc).wait_send()
    all_blocks(2, slab.at[:, pl.ds(0, slab.shape[1] // 2)]).wait_send()


def drain(*refs):
    sems = refs[-1]
    moves = [pltpu.make_async_copy(refs[n], refs[5 + n], sems.at[n]) for n in range(5)]
    for move in moves:
        move.start()
    for move in moves:
        move.wait()


def on_device(pseudo_grads, master_slab, momentum, inner_inputs, token_ids, inner_weight, readout):
    groups = lax.axis_size("island")
    tokens, k = inner_inputs.shape
    r = inner_weight.shape[1]
    features = readout.shape[0]
    g = 4 * r
    width, cols = pseudo_grads.shape[2], master_slab.shape[1]
    out_rows = pseudo_grads.shape[1]
    n = k // 2
    share, back_share = 10 * n // 16, 10 * n // 16
    sa, sb = back_share, n - back_share
    scale = 1.0 / math.sqrt(tokens * lax.axis_size("fsdp"))
    V, sem = pltpu.VMEM, pltpu.SemaphoreType.DMA
    anywhere = pl.BlockSpec(memory_space=pl.ANY)

    def body(*refs):
        kernel(groups, share, back_share, scale, *refs)

    shapes = (
        ((out_rows, width), BF16),
        (master_slab.shape, F32),
        (momentum.shape, F32),
        ((1, r, k), F32),
        ((tokens, k), BF16),
    )
    results = pl.pallas_call(
        body,
        out_shape=tuple(V(*shape) for shape in shapes),
        in_specs=[anywhere] * 7,
        out_specs=[pl.BlockSpec(memory_space=pltpu.VMEM)] * 5,
        scratch_shapes=[
            V((tokens, n), BF16),
            V((tokens, n), BF16),
            V((features, n), BF16),
            V((features, n), F32),
            V((features, n), BF16),
            V((features, tokens), BF16),
            V((tokens, features), BF16),
            V((features, tokens), BF16),
            V((tokens, features), BF16),
            V((tokens, n), BF16),
            V((1, tokens), jnp.int32),
            V((4, g), F32),
            V((features, tokens), F32),
            V((features, tokens), F32),
            V((features, tokens), F32),
            V((4, 2, r, sa), BF16),
            V((2, r, sa), BF16),
            V((2, 2, r, sa), BF16),
            V((2, g // 2, sb), BF16),
            V((2, g, sb), BF16),
            V((2, r, sb), BF16),
            V((r, n), BF16),
            V((8, out_rows, cols), F32),
            V((8, out_rows, cols), F32),
            V((3, 2, out_rows, cols), F32),
            V((out_rows, cols), F32),
            V((out_rows, cols), F32),
            V((out_rows, cols), F32),
            sem((N_SEMS,)),
            sem((N_SEMS,)),
            sem((12,)),
            sem((4,)),
        ],
        compiler_params=pltpu.CompilerParams(
            collective_id=0, has_side_effects=True, vmem_limit_bytes=54 * 2**20
        ),
        name="window",
    )(
        pseudo_grads, master_slab, momentum, inner_inputs, token_ids.reshape(1, tokens),
        inner_weight, readout.reshape(4, g),
    )
    return pl.pallas_call(
        drain,
        out_shape=tuple(jax.ShapeDtypeStruct(*shape) for shape in shapes),
        in_specs=[pl.BlockSpec(memory_space=pltpu.VMEM)] * 5,
        out_specs=[anywhere] * 5,
        scratch_shapes=[sem((5,))],
        compiler_params=pltpu.CompilerParams(vmem_limit_bytes=2**20),
        name="drain",
    )(*(pltpu.with_memory_space_constraint(result, pltpu.VMEM) for result in results))


def solution(mesh):
    in_specs = (
        P("island", "fsdp", None),
        P("fsdp", "island"),
        P("fsdp", "island"),
        P(("island", "fsdp"), None),
        P(("island", "fsdp")),
        P("island", "fsdp", None),
        P(),
    )
    out_specs = (
        P("fsdp", None),
        P("fsdp", "island"),
        P("fsdp", "island"),
        P("island", "fsdp", None),
        P(("island", "fsdp"), None),
    )
    return jax.shard_map(
        on_device, mesh=mesh, in_specs=in_specs, out_specs=out_specs, check_vma=False
    )
```

time: 125 us -> 122 us (0.976)
  Pallas kernels: 122 us -> 119 us
    pallas_call x1, Pallas kernels: 119 us -> 116 us  [on_device(): pl.pallas_call(body, out_shape=tuple((V(*shape) for shape in shapes)), in...]
where the time goes in v4:
time: 122 us; the launch traced here: 120 us
  Pallas kernels  119 us (98%)
    pallas_call x1, Pallas kernels, on_device(): pl.pallas_call(body, out_shape=tuple((V(*shape) for shape in shapes)), in...  116 us
    pallas_call x1, Pallas kernels, on_device(): pl.pallas_call(drain, out_shape=tuple((jax.ShapeDtypeStruct(*shape) for s...  2.78 us

profile of v4, /device:TPU:22, one launch (start us, length us, event | category | flops | bytes accessed | tf_op | source)
XLA Modules:
  0.0 119.7 jit_solution(13427176488746458619)
XLA Ops:
  0.6 116.2 %window.1 = (bf16[16,28672]{1,0:T(8,128)(2,1)S(1)}, f32[16,1792]{1,0:T(8,128)S(1)}, f32[16,1792]{1,0:T(8,128)S(1)}, f32[1,32,8192]{2,1,0:T(8,128)S(1)}, bf16[256,8192]{1,0:T(8,128)(2,1)S(1)}) custom-call(f32[1,16,28672]{2,1,0:T(8,128)} %refs_0_.1, f32[16,1792]{1,0:T(8,128)} %refs_1_.1, f32[16,1792]{1,0:T(8,128)} %refs_2_.1, bf16[256,8192]{1,0:T(8,128)(2,1)} %refs_3_.1, ...), custom_call_target="tpu_custom_call" | custom-call | tf_op jit(solution)/shard_map/window/pallas_call | solution.py:408
  116.9 2.8 %drain.1 = (bf16[16,28672]{1,0:T(8,128)(2,1)}, f32[16,1792]{1,0:T(8,128)}, f32[16,1792]{1,0:T(8,128)}, f32[1,32,8192]{2,1,0:T(8,128)}, bf16[256,8192]{1,0:T(8,128)(2,1)}) custom-call(bf16[16,28672]{1,0:T(8,128)(2,1)S(1)} %get-tuple-element.10.refs_0_, f32[16,1792]{1,0:T(8,128)S(1)} %get-tuple-element.11.refs_1_, f32[16,1792]{1,0:T(8,128)S(1)} %get-tuple-element.12.refs_2_, ...), custom_call_target="tpu_custom_call" | custom-call | tf_op jit(solution)/shard_map/drain/pallas_call | solution.py:455

commit v5 on v4

--- a/solution.py
+++ b/solution.py
@@ -328,14 +328,14 @@
     add(high(3), sa, sb, [ru1.at[1]], "snd")
     send("U3+", snd.at[low(1), SB], ru0.at[0, pl.ds(0, half)], at_h(1))
     send("U3-", snd.at[high(3), SB], ru0.at[1, pl.ds(half, half)], at_h(3))
+    send("T2+", snd.at[rows(1, mate), SA], rt0.at[0, 1], at_h(1))
     dx_mate(0)
     got_ways("T1")
+    add(rows(3, mate), 0, sa, [rt1.at[1]], "snd")
+    send("T3-", snd.at[rows(3, mate), SA], rt0.at[1, 1], at_h(3))
+    send("T2-", snd.at[rows(3, y), SA], rt0.at[1, 0], at_h(3))
     add(rows(1, y), 0, sa, [rt1.at[0]], "snd")
-    add(rows(3, mate), 0, sa, [rt1.at[1]], "snd")
     send("T3+", snd.at[rows(1, y), SA], rt0.at[0, 0], at_h(1))
-    send("T3-", snd.at[rows(3, mate), SA], rt0.at[1, 1], at_h(3))
-    send("T2+", snd.at[rows(1, mate), SA], rt0.at[0, 1], at_h(1))
-    send("T2-", snd.at[rows(3, y), SA], rt0.at[1, 0], at_h(3))
     sum_across(0, "dwp")
     dx_own()
 
@@ -351,19 +351,20 @@
     add(group(0), sa, sb, [ru0.at[0], ru0.at[1]])
     for k, at in enumerate((near, far)):
         send(f"sb{k}", snd.at[rows(0, at), SB], rb.at[k], link)
+    got("T2+", "T3-")
+    add(rows(0, mate), 0, sa, [rt0.at[0, 1], rt0.at[1, 1]], "snd")
+    send("fa", snd.at[rows(0, mate), SA], rs.at[:, SA], pair)
     got("sb0", "sb1")
     add(rows(0, mate), sa, sb, [rb.at[1]], "snd")
     send("fb", snd.at[rows(0, mate), SB], rs.at[:, SB], pair)
     add(mine_rows, sa, sb, [rb.at[0]], "dwp")
-    got_ways("T2", "T3")
-    add(rows(0, mate), 0, sa, [rt0.at[0, 1], rt0.at[1, 1]], "snd")
-    send("fa", snd.at[rows(0, mate), SA], rs.at[:, SA], pair)
-    add(mine_rows, 0, sa, [rt0.at[0, 0], rt0.at[1, 0]], "dwp")
-    wg_out[0, :, wide(base, n)] = dwp[mine_rows, :]
+    wg_out[0, :, wide(base + sa, sb)] = dwp[mine_rows, SB]
     got("fa", "fb")
     wg_out[0, :, wide(mate_base, n)] = rs[...].astype(F32)
     got("dx0", "dx1")
     all_blocks(2, slab.at[:, pl.ds(0, slab.shape[1] // 2)]).wait_recv()
+    got("T3+", "T2-")
+    wg_out[0, :, wide(base, sa)] = dwp[mine_rows, SA] + rt0[0, 0].astype(F32) + rt0[1, 0].astype(F32)
 
     for copy in copies.values():
         copy.wait_send()

time: 122 us -> 120 us (0.984); the launches traced: 120 us -> 119 us
  no operation moved by 1% of the time
where the time goes in v5:
time: 120 us; the launch traced here: 119 us
  Pallas kernels  119 us (99%)
    pallas_call x1, Pallas kernels, on_device(): pl.pallas_call(body, out_shape=tuple((V(*shape) for shape in shapes)), in...  116 us
    pallas_call x1, Pallas kernels, on_device(): pl.pallas_call(drain, out_shape=tuple((jax.ShapeDtypeStruct(*shape) for s...  2.78 us

profile of v5, /device:TPU:22, one launch (start us, length us, event | category | flops | bytes accessed | tf_op | source)
XLA Modules:
  0.0 119.3 jit_solution(4379063977274922700)
XLA Ops:
  0.6 115.9 %window.1 = (bf16[16,28672]{1,0:T(8,128)(2,1)S(1)}, f32[16,1792]{1,0:T(8,128)S(1)}, f32[16,1792]{1,0:T(8,128)S(1)}, f32[1,32,8192]{2,1,0:T(8,128)S(1)}, bf16[256,8192]{1,0:T(8,128)(2,1)S(1)}) custom-call(f32[1,16,28672]{2,1,0:T(8,128)} %refs_0_.1, f32[16,1792]{1,0:T(8,128)} %refs_1_.1, f32[16,1792]{1,0:T(8,128)} %refs_2_.1, bf16[256,8192]{1,0:T(8,128)(2,1)} %refs_3_.1, ...), custom_call_target="tpu_custom_call" | custom-call | tf_op jit(solution)/shard_map/window/pallas_call | solution.py:409
  116.5 2.8 %drain.1 = (bf16[16,28672]{1,0:T(8,128)(2,1)}, f32[16,1792]{1,0:T(8,128)}, f32[16,1792]{1,0:T(8,128)}, f32[1,32,8192]{2,1,0:T(8,128)}, bf16[256,8192]{1,0:T(8,128)(2,1)}) custom-call(bf16[16,28672]{1,0:T(8,128)(2,1)S(1)} %get-tuple-element.10.refs_0_, f32[16,1792]{1,0:T(8,128)S(1)} %get-tuple-element.11.refs_1_, f32[16,1792]{1,0:T(8,128)S(1)} %get-tuple-element.12.refs_2_, ...), custom_call_target="tpu_custom_call" | custom-call | tf_op jit(solution)/shard_map/drain/pallas_call | solution.py:456

commit v6 on v5

--- a/solution.py
+++ b/solution.py
@@ -278,12 +278,12 @@
     across(0, "o")
     slope(1)
     dw(3)
-    dw(1)
+    send("U2-", snd.at[low(3), SB], ru0.at[1, pl.ds(0, half)], at_h(3))
     got_ways("hbf")
-    send("U2+", snd.at[high(1), SB], ru0.at[0, pl.ds(half, half)], at_h(1))
-    send("U2-", snd.at[low(3), SB], ru0.at[1, pl.ds(0, half)], at_h(3))
     across_done(2)
     pre_mate(2)
+    dw(1)
+    send("U2+", snd.at[high(1), SB], ru0.at[0, pl.ds(half, half)], at_h(1))
     pre_own(2)
 
     got("Z")

time: 120 us -> 120 us (level)
  no operation moved by 1% of the time
where the time goes in v6:
time: 120 us; the launch traced here: 118 us
  Pallas kernels  118 us (98%)
    pallas_call x1, Pallas kernels, on_device(): pl.pallas_call(body, out_shape=tuple((V(*shape) for shape in shapes)), in...  115 us
    pallas_call x1, Pallas kernels, on_device(): pl.pallas_call(drain, out_shape=tuple((jax.ShapeDtypeStruct(*shape) for s...  2.78 us

profile of v6, /device:TPU:22, one launch (start us, length us, event | category | flops | bytes accessed | tf_op | source)
XLA Modules:
  0.0 118.3 jit_solution(1094917955481947563)
XLA Ops:
  0.6 114.9 %window.1 = (bf16[16,28672]{1,0:T(8,128)(2,1)S(1)}, f32[16,1792]{1,0:T(8,128)S(1)}, f32[16,1792]{1,0:T(8,128)S(1)}, f32[1,32,8192]{2,1,0:T(8,128)S(1)}, bf16[256,8192]{1,0:T(8,128)(2,1)S(1)}) custom-call(f32[1,16,28672]{2,1,0:T(8,128)} %refs_0_.1, f32[16,1792]{1,0:T(8,128)} %refs_1_.1, f32[16,1792]{1,0:T(8,128)} %refs_2_.1, bf16[256,8192]{1,0:T(8,128)(2,1)} %refs_3_.1, ...), custom_call_target="tpu_custom_call" | custom-call | tf_op jit(solution)/shard_map/window/pallas_call | solution.py:409
  115.6 2.8 %drain.1 = (bf16[16,28672]{1,0:T(8,128)(2,1)}, f32[16,1792]{1,0:T(8,128)}, f32[16,1792]{1,0:T(8,128)}, f32[1,32,8192]{2,1,0:T(8,128)}, bf16[256,8192]{1,0:T(8,128)(2,1)}) custom-call(bf16[16,28672]{1,0:T(8,128)(2,1)S(1)} %get-tuple-element.10.refs_0_, f32[16,1792]{1,0:T(8,128)S(1)} %get-tuple-element.11.refs_1_, f32[16,1792]{1,0:T(8,128)S(1)} %get-tuple-element.12.refs_2_, ...), custom_call_target="tpu_custom_call" | custom-call | tf_op jit(solution)/shard_map/drain/pallas_call | solution.py:456

commit v7 on v5

--- a/solution.py
+++ b/solution.py
@@ -159,8 +159,12 @@
         send(f"s{d}", slt.at[group(d)], spt.at[group(d)], pair)
         slo[:, group(d)] = jnp.transpose(value).astype(BF16)
 
-    def dw(d):
-        got(f"s{d}")
+    def turn(d):
+        sp[:, group(d)] = jnp.transpose(spt[group(d)].astype(F32)).astype(BF16)
+
+    def dw(d, wait=True):
+        if wait:
+            got(f"s{d}")
         own, other = slt[group(d)], spt[group(d)]
 
         def body(j, carry):
@@ -306,11 +310,14 @@
     across_back(3)
     pre_own(0)
     slope(0)
-    dw(0)
-    across_back(0)
+    for d in (1, 3, 2):
+        turn(d)
     sum_across(2)
     send("T1+", snd.at[rows(2, y), SA], rt1.at[0], at_h(1))
     send("T1-", snd.at[rows(2, mate), SA], rt1.at[1], at_h(3))
+    got("s0")
+    turn(0)
+    dx_mate(1)
 
     got("SZ")
     other = block(x * 4 + (1 - z) * 2 + c)
@@ -318,11 +325,7 @@
         send(f"SX{d}", slab.at[:, mine], slab.at[:, mine], at_x(d))
         send(f"SY{d}", slab.at[:, other], slab.at[:, other], at_x(d))
 
-    sum_across(3)
     sum_across(1)
-    for d in range(4):
-        sp[:, group(d)] = jnp.transpose(spt[group(d)].astype(F32)).astype(BF16)
-    dx_mate(1)
     got_ways("U1")
     add(low(1), sa, sb, [ru1.at[0]], "snd")
     add(high(3), sa, sb, [ru1.at[1]], "snd")
@@ -330,6 +333,9 @@
     send("U3-", snd.at[high(3), SB], ru0.at[1, pl.ds(half, half)], at_h(3))
     send("T2+", snd.at[rows(1, mate), SA], rt0.at[0, 1], at_h(1))
     dx_mate(0)
+    dw(0, False)
+    across_back(0)
+    sum_across(3)
     got_ways("T1")
     add(rows(3, mate), 0, sa, [rt1.at[1]], "snd")
     send("T3-", snd.at[rows(3, mate), SA], rt0.at[1, 1], at_h(3))
@@ -374,7 +380,11 @@
 
 def drain(*refs):
     sems = refs[-1]
-    moves = [pltpu.make_async_copy(refs[n], refs[5 + n], sems.at[n]) for n in range(5)]
+    moves = [pltpu.make_async_copy(refs[n], refs[5 + n], sems.at[n]) for n in range(4)]
+    part = refs[4].shape[0] // 4
+    for n in range(4):
+        at = pl.ds(n * part, part)
+        moves.insert(n, pltpu.make_async_copy(refs[4].at[at], refs[9].at[at], sems.at[4 + n]))
     for move in moves:
         move.start()
     for move in moves:
@@ -390,7 +400,7 @@
     width, cols = pseudo_grads.shape[2], master_slab.shape[1]
     out_rows = pseudo_grads.shape[1]
     n = k // 2
-    share, back_share = 10 * n // 16, 10 * n // 16
+    share, back_share = 10 * n // 16, 21 * n // 32
     sa, sb = back_share, n - back_share
     scale = 1.0 / math.sqrt(tokens * lax.axis_size("fsdp"))
     V, sem = pltpu.VMEM, pltpu.SemaphoreType.DMA
@@ -458,7 +468,7 @@
         out_shape=tuple(jax.ShapeDtypeStruct(*shape) for shape in shapes),
         in_specs=[pl.BlockSpec(memory_space=pltpu.VMEM)] * 5,
         out_specs=[anywhere] * 5,
-        scratch_shapes=[sem((5,))],
+        scratch_shapes=[sem((8,))],
         compiler_params=pltpu.CompilerParams(vmem_limit_bytes=2**20),
         name="drain",
     )(*(pltpu.with_memory_space_constraint(result, pltpu.VMEM) for result in results))

time: 120 us -> 121 us (level)
  no operation moved by 1% of the time
where the time goes in v7:
time: 121 us; the launch traced here: 120 us
  Pallas kernels  119 us (98%)
    pallas_call x1, Pallas kernels, on_device(): pl.pallas_call(body, out_shape=tuple((V(*shape) for shape in shapes)), in...  116 us
    pallas_call x1, Pallas kernels, on_device(): pl.pallas_call(drain, out_shape=tuple((jax.ShapeDtypeStruct(*shape) for s...  2.77 us

profile of v7, /device:TPU:22, one launch (start us, length us, event | category | flops | bytes accessed | tf_op | source)
XLA Modules:
  0.0 119.8 jit_solution(16156986801381919831)
XLA Ops:
  0.6 116.3 %window.1 = (bf16[16,28672]{1,0:T(8,128)(2,1)S(1)}, f32[16,1792]{1,0:T(8,128)S(1)}, f32[16,1792]{1,0:T(8,128)S(1)}, f32[1,32,8192]{2,1,0:T(8,128)S(1)}, bf16[256,8192]{1,0:T(8,128)(2,1)S(1)}) custom-call(f32[1,16,28672]{2,1,0:T(8,128)} %refs_0_.1, f32[16,1792]{1,0:T(8,128)} %refs_1_.1, f32[16,1792]{1,0:T(8,128)} %refs_2_.1, bf16[256,8192]{1,0:T(8,128)(2,1)} %refs_3_.1, ...), custom_call_target="tpu_custom_call" | custom-call | tf_op jit(solution)/shard_map/window/pallas_call | solution.py:419
  117.0 2.8 %drain.1 = (bf16[16,28672]{1,0:T(8,128)(2,1)}, f32[16,1792]{1,0:T(8,128)}, f32[16,1792]{1,0:T(8,128)}, f32[1,32,8192]{2,1,0:T(8,128)}, bf16[256,8192]{1,0:T(8,128)(2,1)}) custom-call(bf16[16,28672]{1,0:T(8,128)(2,1)S(1)} %get-tuple-element.10.refs_0_, f32[16,1792]{1,0:T(8,128)S(1)} %get-tuple-element.11.refs_1_, f32[16,1792]{1,0:T(8,128)S(1)} %get-tuple-element.12.refs_2_, ...), custom_call_target="tpu_custom_call" | custom-call | tf_op jit(solution)/shard_map/drain/pallas_call | solution.py:466
